TPU v7x, 32 devices: a whole 2x2x4 slice. The times are simulated.
32 devices in a mesh: grp: 2 (over x), seq: 16 (over z, y, core).
Axes of the slice: x: 2, y: 2, z: 4, core: 2. Of those that a mesh axis runs over, the one named last changes fastest.
Arguments:
- query_inputs: bfloat16 [32768, 128], P(('grp', 'seq')), parts along dimension 0, may hold values from -6 to 6
- key_inputs: bfloat16 [32768, 128], P(('grp', 'seq')), parts along dimension 0, may hold values from -5.3 to 4.8
- value_inputs: bfloat16 [32768, 2048], P(('grp', 'seq')), parts along dimension 0, may hold values from -5.3 to 4.8
- log_decay: float32 [16, 32768], P(None, ('grp', 'seq')), parts along dimension 1, may hold values from -0.9 to 0, as said below
- level_weight: bfloat16 [15, 16, 32768], P(None, None, ('grp', 'seq')), parts along dimension 2, may hold values from 0.099609375 to 1
- conv_weight: float32 [4, 2304], replicated, may hold values from 0.35 to 0.65
- norm_gain: float32 [2048], replicated, may hold values from 0.1 to 1.9
Outputs:
- mixer_out: bfloat16 [32768, 2048], P(('grp', 'seq')), parts along dimension 0
There are 2 independent parts, one for each index of `grp`. A program takes and returns all parts, laid end to end along the dimension named above; an argument that names none is the same for every part. Nothing has to cross between parts.
Inputs may be any that keep to these rules, and one draw needn't show every extreme that they name: `log_decay`: each entry is the logarithm of one head's decay factor at one token.
All inputs are finite; a program needn't handle non-finite values.
Results may differ from a plain program's by a relative error of at most 0.014.
Values may be sent and summed in bfloat16 or wider, within the bound.
A program may use at most 64 MiB of HBM per device.

v0:
```python
import jax
import jax.numpy as jnp
from jax import lax
from jax.sharding import PartitionSpec as P

EPSILON = 1e-05


def partner(x, axis, distance):
    return lax.ppermute(x, axis, [(i, i ^ 1 << distance) for i in range(lax.axis_size(axis))])


def from_behind(x, axis, by):
    size = lax.axis_size(axis)
    pairs = [(i, i + by) for i in range(size) if 0 <= i + by < size]
    return lax.ppermute(x, axis, pairs)


def causal_conv(current, previous, weight):
    length = current.shape[0]
    tap_count = weight.shape[0]
    joined = jnp.concatenate([previous, current], axis=0).astype(jnp.float32)
    summed = jnp.zeros(current.shape, jnp.float32)
    for tap_pos in range(tap_count):
        summed = summed + weight[tap_pos][None, :] * joined[tap_pos : tap_pos + length]
    return jax.nn.silu(summed).astype(jnp.bfloat16)


def level_of(length, bit_count):
    position_list = lax.iota(jnp.int32, length)
    differ = jnp.bitwise_xor(position_list[:, None], position_list[None, :])
    levels = jnp.zeros((length, length), jnp.int32)
    for bit_pos in range(bit_count):
        levels = levels + (differ >= 1 << bit_pos).astype(jnp.int32)
    return (levels, position_list[:, None] >= position_list[None, :])


def climb(group_state, shard_total, shard_index, bit_count):
    block_state = group_state
    block_total = shard_total
    offset = jnp.zeros_like(shard_total)
    buckets = []
    for bit_pos in range(bit_count):
        other_state, other_total = partner((block_state, block_total), "seq", bit_pos)
        upper_half = shard_index >> bit_pos & 1 == 1
        lifted = jnp.exp(offset)[:, None, None] * other_state
        buckets.append(jnp.where(upper_half, lifted, 0.0).astype(jnp.bfloat16))
        if bit_pos + 1 < bit_count:
            block_state = jnp.where(
                upper_half,
                block_state + jnp.exp(block_total)[:, None, None] * other_state,
                other_state + jnp.exp(other_total)[:, None, None] * block_state,
            )
            block_total = block_total + other_total
            offset = offset + jnp.where(upper_half, other_total, 0.0)
    return jnp.stack(buckets, axis=0)


def on_device(
    query_inputs, key_inputs, value_inputs, log_decay, level_weight, conv_weight, norm_gain
):
    length = query_inputs.shape[0]
    state_dim = query_inputs.shape[1]
    head_count = log_decay.shape[0]
    head_width = value_inputs.shape[1] // head_count
    rim_width = conv_weight.shape[0] - 1
    seq_bits = lax.axis_size("seq").bit_length() - 1
    token_bits = length.bit_length() - 1
    shard_index = lax.axis_index("seq")
    rim_parts = from_behind(
        (
            query_inputs[length - rim_width :],
            key_inputs[length - rim_width :],
            value_inputs[length - rim_width :],
        ),
        "seq",
        1,
    )
    queries = causal_conv(query_inputs, rim_parts[0], conv_weight[:, :state_dim])
    keys_conv = causal_conv(key_inputs, rim_parts[1], conv_weight[:, state_dim : 2 * state_dim])
    values_conv = causal_conv(value_inputs, rim_parts[2], conv_weight[:, 2 * state_dim :])
    cumul_decay = jnp.cumsum(log_decay, axis=1)
    shard_total = cumul_decay[:, length - 1]
    tail_decay = jnp.exp(shard_total[:, None] - cumul_decay)
    decayed = (keys_conv.astype(jnp.float32)[None, :, :] * tail_decay[:, :, None]).astype(
        jnp.bfloat16
    )
    value_heads = values_conv.reshape(length, head_count, head_width)
    group_state = jnp.einsum(
        "hcn,chp->hnp", decayed, value_heads, preferred_element_type=jnp.float32
    )
    scores = lax.dot_general(
        queries, keys_conv, (((1,), (1,)), ((), ())), preferred_element_type=jnp.float32
    )
    near_levels = level_weight[: token_bits + 1]
    far_levels = level_weight[token_bits + 1 :]
    query_float = queries.astype(jnp.float32)
    levels, causal = level_of(length, token_bits)

    def near_part(head_idx):
        decay_row = lax.dynamic_index_in_dim(cumul_decay, head_idx, 0, keepdims=False)
        weights_row = lax.dynamic_index_in_dim(near_levels, head_idx, 1, keepdims=False).astype(
            jnp.float32
        )
        mixing = jnp.zeros((length, length), jnp.float32)
        for level_pos in range(token_bits + 1):
            mixing = mixing + jnp.where(levels == level_pos, weights_row[level_pos][:, None], 0.0)
        decay_gap = jnp.where(causal, decay_row[:, None] - decay_row[None, :], -1e30)
        near_weight = (scores * mixing * jnp.exp(decay_gap)).astype(jnp.bfloat16)
        own_values = lax.dynamic_slice_in_dim(values_conv, head_idx * head_width, head_width, 1)
        return jnp.dot(near_weight, own_values, preferred_element_type=jnp.float32)

    def far_part(head_idx, buckets):
        decay_row = lax.dynamic_index_in_dim(cumul_decay, head_idx, 0, keepdims=False)
        far_scale = (
            lax.dynamic_index_in_dim(far_levels, head_idx, 1, keepdims=False).astype(jnp.float32)
            * jnp.exp(decay_row)[None, :]
        )
        far_query = (
            (query_float[:, None, :] * far_scale.T[:, :, None])
            .astype(jnp.bfloat16)
            .reshape(length, seq_bits * state_dim)
        )
        head_buckets = lax.dynamic_index_in_dim(buckets, head_idx, 1, keepdims=False).reshape(
            seq_bits * state_dim, head_width
        )
        return jnp.dot(far_query, head_buckets, preferred_element_type=jnp.float32)

    def finish(head_idx, pre_norm, output):
        gain_row = lax.dynamic_slice_in_dim(norm_gain, head_idx * head_width, head_width, 0)
        normed = (
            pre_norm
            * lax.rsqrt(jnp.mean(pre_norm * pre_norm, axis=1, keepdims=True) + EPSILON)
            * gain_row[None, :]
        )
        return lax.dynamic_update_slice_in_dim(
            output, normed.astype(jnp.bfloat16), head_idx * head_width, 1
        )

    blank_out = jnp.zeros((length, head_count * head_width), jnp.bfloat16)

    def near_step(head_idx, near_all):
        return lax.dynamic_update_slice_in_dim(
            near_all, near_part(head_idx), head_idx * head_width, 1
        )

    near_all = lax.fori_loop(
        0, head_count, near_step, jnp.zeros((length, head_count * head_width), jnp.float32)
    )
    buckets = climb(group_state, shard_total, shard_index, seq_bits)

    def far_step(head_idx, output):
        near_term = lax.dynamic_slice_in_dim(near_all, head_idx * head_width, head_width, 1)
        return finish(head_idx, near_term + far_part(head_idx, buckets), output)

    return lax.fori_loop(0, head_count, far_step, blank_out)


def solution(mesh):
    return jax.shard_map(
        on_device,
        mesh=mesh,
        in_specs=(
            P(("grp", "seq"), None),
            P(("grp", "seq"), None),
            P(("grp", "seq"), None),
            P(None, ("grp", "seq")),
            P(None, None, ("grp", "seq")),
            P(),
            P(),
        ),
        out_specs=P(("grp", "seq"), None),
        check_vma=False,
    )
```

profile of v0, /device:TPU:0, one launch (start us, length us, event | category | flops | bytes accessed | tf_op | source)
XLA Modules:
  0.0 439.1 jit_solution(3361163196439672587)
XLA Ops:
  0.7 2.3 collective-permute-start.1
  3.8 4.5 %collective-permute-start.2 = (bf16[3,2048]{1,0:T(4,128)(2,1)S(1)}, bf16[3,2048]{1,0:T(4,128)(2,1)S(1)}, u32[]{:S(2)}, u32[]{:S(2)}) collective-permute-start(bf16[3,2048]{1,0:T(4,128)(2,1)S(1)} %slice.223), channel_id=1, source_target_pairs={{0,1},{1,2},{2,3},{3,4},{4,5},{5,6},{6,7},{7,8},{8,9},{9,10},{10,1... | collective-permute-start | bytes 36872 | tf_op jit(solution)/shard_map/ppermute | solution.py:16
  9.2 4.5 %reduce-window.6 = f32[16,8,128]{2,1,0:T(8,128)S(1)} reduce-window(f32[16,8,128]{2,1,0:T(8,128)S(1)} %bitcast.116, f32[]{:T(128)} %constant.201.clone.1), window={size=1x1x128 pad=0_0x0_0x127_0}, to_apply=%region_0.1 | reduce-window | flops 2080768 | bytes 131076 | tf_op jit(solution)/shard_map/reduce-window
  17.8 3.4 maximum_convert_fusion
  21.2 5.9 %fusion.42 = f32[16,128,128]{2,1,0:T(8,128)S(1)} fusion(f32[16,1024]{1,0:T(8,128)S(1)} %subtract_exponential_fusion, f32[1024,128]{0,1:T(8,128)S(1)} %copy.18, f32[1027,2048]{1,0:T(8,128)S(1)} %maximum_convert_fusion, f32[2048]{0:T(1024)S(1)} %bitcast.136, f32[2048]{0:T(1024)S(1)} %bitcast.138, f32[2048]{0:T(1024)S(1)} %bitcast.134, f32[2048]{0:T(1024)S(1)} %bitcast.132), kind=kOutput, calls=%fused_computation.64 | convolution fusion | flops 566231040 | bytes 35225600 | tf_op jit(solution)/shard_map/hcn,chp->hnp/dot_general | solution.py:89
  27.7 2.2 collective-permute-start
  31.4 2.0 collective-permute-done.6
  33.5 1.6 collective-permute-start.8
  37.5 2.8 fusion.68
  40.3 20.3 %collective-permute-done.5 = f32[16,128,128]{2,1,0:T(8,128)S(1)} collective-permute-done((f32[16,128,128]{2,1,0:T(8,128)S(1)}, f32[16,128,128]{2,1,0:T(8,128)S(1)}, u32[]{:S(2)}, u32[]{:S(2)}) %collective-permute-start.5) | collective-permute-done | bytes 1048608 | tf_op jit(solution)/shard_map/ppermute | solution.py:10
  61.6 6.4 %multiply_convert_fusion.7 = bf16[1024,2048]{1,0:T(8,128)(2,1)} fusion(f32[1027,2048]{1,0:T(8,128)S(1)} %copy-done.1, f32[2048]{0:T(1024)S(1)} %bitcast.137, f32[2048]{0:T(1024)S(1)} %bitcast.139, f32[2048]{0:T(1024)S(1)} %bitcast.135, f32[2048]{0:T(1024)S(1)} %bitcast.133), kind=kLoop, calls=%fused_computation.62 | loop fusion | flops 25165824 | bytes 37781504 | tf_op jit(solution)/shard_map/convert_element_type | solution.py:26
  68.0 17.5 %collective-permute-done.7 = f32[16,128,128]{2,1,0:T(8,128)S(1)} collective-permute-done((f32[16,128,128]{2,1,0:T(8,128)S(1)}, f32[16,128,128]{2,1,0:T(8,128)S(1)}, u32[]{:S(2)}, u32[]{:S(2)}) %collective-permute-start.7) | collective-permute-done | bytes 1048608 | tf_op jit(solution)/shard_map/ppermute | solution.py:10
  88.2 4.3 broadcast_in_dim.270
  92.5 201.8 %while.29 = (s32[]{:T(128)}, f32[1024,2048]{1,0:T(8,128)}, bf16[11,16,1024]{2,1,0:T(8,128)(2,1)S(1)}, f32[1024,1024]{1,0:T(8,128)}, f32[16,1024]{1,0:T(8,128)S(1...) while((s32[]{:T(128)}, f32[1024,2048]{1,0:T(8,128)}, ...), condition=%wide.region_3.4_spmd.clone.clone, body=%wide.region_2.3_spmd.clone.clone.sunk | while | flops 339749888 | bytes 5201051 | solution.py:147
  92.6 12.5 %fusion.84 = f32[1024,2048]{1,0:T(8,128)} fusion(f32[1024,2048]{1,0:T(8,128)} %get-tuple-element.571, s32[]{:T(128)S(6)} %select_n.350, f32[1024,1024]{1,0:T(8,128)} %get-tuple-element.583, f32[1024]{0:T(1024)S(1)} %bitcast.130, f32[1024]{0:T(1024)S(1)} %bitcast.120, f32[1024]{0:T(1024)S(1)} %bitcast.121, f32[1024]{0:T(1024)S(1)} %bitcast.122, ...), kind=kOutput, calls=%fused_computation.31.clone.1 | convolution fusion | flops 339738624 | bytes 5035008 | tf_op jit(solution)/shard_map/while/body/eval_jaxpr/dot_general | solution.py:111
  105.2 12.5 %fusion.84 = f32[1024,2048]{1,0:T(8,128)} fusion(f32[1024,2048]{1,0:T(8,128)} %get-tuple-element.571, s32[]{:T(128)S(6)} %select_n.350, f32[1024,1024]{1,0:T(8,128)} %get-tuple-element.583, f32[1024]{0:T(1024)S(1)} %bitcast.130, f32[1024]{0:T(1024)S(1)} %bitcast.120, f32[1024]{0:T(1024)S(1)} %bitcast.121, f32[1024]{0:T(1024)S(1)} %bitcast.122, ...), kind=kOutput, calls=%fused_computation.31.clone.1 | convolution fusion | flops 339738624 | bytes 5035008 | tf_op jit(solution)/shard_map/while/body/eval_jaxpr/dot_general | solution.py:111
  117.8 12.5 %fusion.84 = f32[1024,2048]{1,0:T(8,128)} fusion(f32[1024,2048]{1,0:T(8,128)} %get-tuple-element.571, s32[]{:T(128)S(6)} %select_n.350, f32[1024,1024]{1,0:T(8,128)} %get-tuple-element.583, f32[1024]{0:T(1024)S(1)} %bitcast.130, f32[1024]{0:T(1024)S(1)} %bitcast.120, f32[1024]{0:T(1024)S(1)} %bitcast.121, f32[1024]{0:T(1024)S(1)} %bitcast.122, ...), kind=kOutput, calls=%fused_computation.31.clone.1 | convolution fusion | flops 339738624 | bytes 5035008 | tf_op jit(solution)/shard_map/while/body/eval_jaxpr/dot_general | solution.py:111
  130.4 12.5 %fusion.84 = f32[1024,2048]{1,0:T(8,128)} fusion(f32[1024,2048]{1,0:T(8,128)} %get-tuple-element.571, s32[]{:T(128)S(6)} %select_n.350, f32[1024,1024]{1,0:T(8,128)} %get-tuple-element.583, f32[1024]{0:T(1024)S(1)} %bitcast.130, f32[1024]{0:T(1024)S(1)} %bitcast.120, f32[1024]{0:T(1024)S(1)} %bitcast.121, f32[1024]{0:T(1024)S(1)} %bitcast.122, ...), kind=kOutput, calls=%fused_computation.31.clone.1 | convolution fusion | flops 339738624 | bytes 5035008 | tf_op jit(solution)/shard_map/while/body/eval_jaxpr/dot_general | solution.py:111
  143.0 12.5 %fusion.84 = f32[1024,2048]{1,0:T(8,128)} fusion(f32[1024,2048]{1,0:T(8,128)} %get-tuple-element.571, s32[]{:T(128)S(6)} %select_n.350, f32[1024,1024]{1,0:T(8,128)} %get-tuple-element.583, f32[1024]{0:T(1024)S(1)} %bitcast.130, f32[1024]{0:T(1024)S(1)} %bitcast.120, f32[1024]{0:T(1024)S(1)} %bitcast.121, f32[1024]{0:T(1024)S(1)} %bitcast.122, ...), kind=kOutput, calls=%fused_computation.31.clone.1 | convolution fusion | flops 339738624 | bytes 5035008 | tf_op jit(solution)/shard_map/while/body/eval_jaxpr/dot_general | solution.py:111
  155.7 12.5 %fusion.84 = f32[1024,2048]{1,0:T(8,128)} fusion(f32[1024,2048]{1,0:T(8,128)} %get-tuple-element.571, s32[]{:T(128)S(6)} %select_n.350, f32[1024,1024]{1,0:T(8,128)} %get-tuple-element.583, f32[1024]{0:T(1024)S(1)} %bitcast.130, f32[1024]{0:T(1024)S(1)} %bitcast.120, f32[1024]{0:T(1024)S(1)} %bitcast.121, f32[1024]{0:T(1024)S(1)} %bitcast.122, ...), kind=kOutput, calls=%fused_computation.31.clone.1 | convolution fusion | flops 339738624 | bytes 5035008 | tf_op jit(solution)/shard_map/while/body/eval_jaxpr/dot_general | solution.py:111
  168.3 12.5 %fusion.84 = f32[1024,2048]{1,0:T(8,128)} fusion(f32[1024,2048]{1,0:T(8,128)} %get-tuple-element.571, s32[]{:T(128)S(6)} %select_n.350, f32[1024,1024]{1,0:T(8,128)} %get-tuple-element.583, f32[1024]{0:T(1024)S(1)} %bitcast.130, f32[1024]{0:T(1024)S(1)} %bitcast.120, f32[1024]{0:T(1024)S(1)} %bitcast.121, f32[1024]{0:T(1024)S(1)} %bitcast.122, ...), kind=kOutput, calls=%fused_computation.31.clone.1 | convolution fusion | flops 339738624 | bytes 5035008 | tf_op jit(solution)/shard_map/while/body/eval_jaxpr/dot_general | solution.py:111
  180.9 12.5 %fusion.84 = f32[1024,2048]{1,0:T(8,128)} fusion(f32[1024,2048]{1,0:T(8,128)} %get-tuple-element.571, s32[]{:T(128)S(6)} %select_n.350, f32[1024,1024]{1,0:T(8,128)} %get-tuple-element.583, f32[1024]{0:T(1024)S(1)} %bitcast.130, f32[1024]{0:T(1024)S(1)} %bitcast.120, f32[1024]{0:T(1024)S(1)} %bitcast.121, f32[1024]{0:T(1024)S(1)} %bitcast.122, ...), kind=kOutput, calls=%fused_computation.31.clone.1 | convolution fusion | flops 339738624 | bytes 5035008 | tf_op jit(solution)/shard_map/while/body/eval_jaxpr/dot_general | solution.py:111
  193.5 12.6 %fusion.84 = f32[1024,2048]{1,0:T(8,128)} fusion(f32[1024,2048]{1,0:T(8,128)} %get-tuple-element.571, s32[]{:T(128)S(6)} %select_n.350, f32[1024,1024]{1,0:T(8,128)} %get-tuple-element.583, f32[1024]{0:T(1024)S(1)} %bitcast.130, f32[1024]{0:T(1024)S(1)} %bitcast.120, f32[1024]{0:T(1024)S(1)} %bitcast.121, f32[1024]{0:T(1024)S(1)} %bitcast.122, ...), kind=kOutput, calls=%fused_computation.31.clone.1 | convolution fusion | flops 339738624 | bytes 5035008 | tf_op jit(solution)/shard_map/while/body/eval_jaxpr/dot_general | solution.py:111
  206.1 12.5 %fusion.84 = f32[1024,2048]{1,0:T(8,128)} fusion(f32[1024,2048]{1,0:T(8,128)} %get-tuple-element.571, s32[]{:T(128)S(6)} %select_n.350, f32[1024,1024]{1,0:T(8,128)} %get-tuple-element.583, f32[1024]{0:T(1024)S(1)} %bitcast.130, f32[1024]{0:T(1024)S(1)} %bitcast.120, f32[1024]{0:T(1024)S(1)} %bitcast.121, f32[1024]{0:T(1024)S(1)} %bitcast.122, ...), kind=kOutput, calls=%fused_computation.31.clone.1 | convolution fusion | flops 339738624 | bytes 5035008 | tf_op jit(solution)/shard_map/while/body/eval_jaxpr/dot_general | solution.py:111
  218.7 12.5 %fusion.84 = f32[1024,2048]{1,0:T(8,128)} fusion(f32[1024,2048]{1,0:T(8,128)} %get-tuple-element.571, s32[]{:T(128)S(6)} %select_n.350, f32[1024,1024]{1,0:T(8,128)} %get-tuple-element.583, f32[1024]{0:T(1024)S(1)} %bitcast.130, f32[1024]{0:T(1024)S(1)} %bitcast.120, f32[1024]{0:T(1024)S(1)} %bitcast.121, f32[1024]{0:T(1024)S(1)} %bitcast.122, ...), kind=kOutput, calls=%fused_computation.31.clone.1 | convolution fusion | flops 339738624 | bytes 5035008 | tf_op jit(solution)/shard_map/while/body/eval_jaxpr/dot_general | solution.py:111
  231.3 12.6 %fusion.84 = f32[1024,2048]{1,0:T(8,128)} fusion(f32[1024,2048]{1,0:T(8,128)} %get-tuple-element.571, s32[]{:T(128)S(6)} %select_n.350, f32[1024,1024]{1,0:T(8,128)} %get-tuple-element.583, f32[1024]{0:T(1024)S(1)} %bitcast.130, f32[1024]{0:T(1024)S(1)} %bitcast.120, f32[1024]{0:T(1024)S(1)} %bitcast.121, f32[1024]{0:T(1024)S(1)} %bitcast.122, ...), kind=kOutput, calls=%fused_computation.31.clone.1 | convolution fusion | flops 339738624 | bytes 5035008 | tf_op jit(solution)/shard_map/while/body/eval_jaxpr/dot_general | solution.py:111
  244.0 12.5 %fusion.84 = f32[1024,2048]{1,0:T(8,128)} fusion(f32[1024,2048]{1,0:T(8,128)} %get-tuple-element.571, s32[]{:T(128)S(6)} %select_n.350, f32[1024,1024]{1,0:T(8,128)} %get-tuple-element.583, f32[1024]{0:T(1024)S(1)} %bitcast.130, f32[1024]{0:T(1024)S(1)} %bitcast.120, f32[1024]{0:T(1024)S(1)} %bitcast.121, f32[1024]{0:T(1024)S(1)} %bitcast.122, ...), kind=kOutput, calls=%fused_computation.31.clone.1 | convolution fusion | flops 339738624 | bytes 5035008 | tf_op jit(solution)/shard_map/while/body/eval_jaxpr/dot_general | solution.py:111
  256.6 12.5 %fusion.84 = f32[1024,2048]{1,0:T(8,128)} fusion(f32[1024,2048]{1,0:T(8,128)} %get-tuple-element.571, s32[]{:T(128)S(6)} %select_n.350, f32[1024,1024]{1,0:T(8,128)} %get-tuple-element.583, f32[1024]{0:T(1024)S(1)} %bitcast.130, f32[1024]{0:T(1024)S(1)} %bitcast.120, f32[1024]{0:T(1024)S(1)} %bitcast.121, f32[1024]{0:T(1024)S(1)} %bitcast.122, ...), kind=kOutput, calls=%fused_computation.31.clone.1 | convolution fusion | flops 339738624 | bytes 5035008 | tf_op jit(solution)/shard_map/while/body/eval_jaxpr/dot_general | solution.py:111
  269.2 12.5 %fusion.84 = f32[1024,2048]{1,0:T(8,128)} fusion(f32[1024,2048]{1,0:T(8,128)} %get-tuple-element.571, s32[]{:T(128)S(6)} %select_n.350, f32[1024,1024]{1,0:T(8,128)} %get-tuple-element.583, f32[1024]{0:T(1024)S(1)} %bitcast.130, f32[1024]{0:T(1024)S(1)} %bitcast.120, f32[1024]{0:T(1024)S(1)} %bitcast.121, f32[1024]{0:T(1024)S(1)} %bitcast.122, ...), kind=kOutput, calls=%fused_computation.31.clone.1 | convolution fusion | flops 339738624 | bytes 5035008 | tf_op jit(solution)/shard_map/while/body/eval_jaxpr/dot_general | solution.py:111
  281.8 12.5 %fusion.84 = f32[1024,2048]{1,0:T(8,128)} fusion(f32[1024,2048]{1,0:T(8,128)} %get-tuple-element.571, s32[]{:T(128)S(6)} %select_n.350, f32[1024,1024]{1,0:T(8,128)} %get-tuple-element.583, f32[1024]{0:T(1024)S(1)} %bitcast.130, f32[1024]{0:T(1024)S(1)} %bitcast.120, f32[1024]{0:T(1024)S(1)} %bitcast.121, f32[1024]{0:T(1024)S(1)} %bitcast.122, ...), kind=kOutput, calls=%fused_computation.31.clone.1 | convolution fusion | flops 339738624 | bytes 5035008 | tf_op jit(solution)/shard_map/while/body/eval_jaxpr/dot_general | solution.py:111
  297.6 2.5 broadcast_in_dim.269.clone
  300.1 139.0 %while.28 = (s32[]{:T(128)}, bf16[1024,2048]{1,0:T(8,128)(2,1)}, f32[1024,2048]{1,0:T(8,128)}, f32[1024,128]{1,0:T(8,128)S(1)}, bf16[4,16,1024]{2,1,0:T(8,128)(2...) while((s32[]{:T(128)}, bf16[1024,2048]{1,0:T(8,128)(2,1)}, ...), condition=%wide.region_6.7_spmd, body=%wide.region_4.6_spmd.sunk | while | flops 136061952 | bytes 8132283 | solution.py:156
  301.7 3.9 multiply_convert_fusion.15
  310.4 3.9 multiply_convert_fusion.15
  319.1 3.9 multiply_convert_fusion.15
  327.8 3.9 multiply_convert_fusion.15
  336.4 3.9 multiply_convert_fusion.15
  345.1 3.9 multiply_convert_fusion.15
  353.8 3.9 multiply_convert_fusion.15
  362.5 3.9 multiply_convert_fusion.15
  371.2 3.9 multiply_convert_fusion.15
  379.9 3.9 multiply_convert_fusion.15
  388.6 3.9 multiply_convert_fusion.15
  397.3 3.9 multiply_convert_fusion.15
  406.0 3.9 multiply_convert_fusion.15
  414.7 3.9 multiply_convert_fusion.15
  423.3 3.9 multiply_convert_fusion.15
  432.0 3.9 multiply_convert_fusion.15
  (308 shorter events, 94.4 us)
Async XLA Ops:
  0.7 15.6 %collective-permute-start.1 = (bf16[3,128]{1,0:T(4,128)(2,1)S(1)}, bf16[3,128]{1,0:T(4,128)(2,1)S(1)}, u32[]{:S(2)}, u32[]{:S(2)}) collective-permute-start(bf16[3,128]{1,0:T(4,128)(2,1)S(1)} %slice.212), channel_id=1, source_target_pairs={{0,1},{1,2},{2,3},{3,4},{4,5},{5,6},{6,7},{7,8},{8,9},{9,10},{10,1... | collective-permute-start | bytes 2312 | tf_op jit(solution)/shard_map/ppermute | solution.py:16
  3.8 13.9 %collective-permute-start.2 = (bf16[3,2048]{1,0:T(4,128)(2,1)S(1)}, bf16[3,2048]{1,0:T(4,128)(2,1)S(1)}, u32[]{:S(2)}, u32[]{:S(2)}) collective-permute-start(bf16[3,2048]{1,0:T(4,128)(2,1)S(1)} %slice.223), channel_id=1, source_target_pairs={{0,1},{1,2},{2,3},{3,4},{4,5},{5,6},{6,7},{7,8},{8,9},{9,10},{10,1... | collective-permute-start | bytes 36872 | tf_op jit(solution)/shard_map/ppermute | solution.py:16
  21.2 5.9 %copy-start = (f32[1027,2048]{1,0:T(8,128)}, f32[1027,2048]{1,0:T(8,128)S(1)}, u32[]{:S(2)}) copy-start(f32[1027,2048]{1,0:T(8,128)S(1)} %maximum_convert_fusion) | copy-start | bytes 25239556
  21.2 6.5 %copy-start.2 = (bf16[1024,128]{1,0:T(8,128)(2,1)S(1)}, bf16[1024,128]{1,0:T(8,128)(2,1)}, u32[]{:S(2)}) copy-start(bf16[1024,128]{1,0:T(8,128)(2,1)} %param.11) | copy-start | bytes 786436
  27.1 8.1 %collective-permute-start.3 = (f32[16,128,128]{2,1,0:T(8,128)S(1)}, f32[16,128,128]{2,1,0:T(8,128)S(1)}, u32[]{:S(2)}, u32[]{:S(2)}) collective-permute-start(f32[16,128,128]{2,1,0:T(8,128)S(1)} %fusion.42), channel_id=1, source_target_pairs={{0,1},{1,0},{2,3},{3,2},{4,5},{5,4},{6,7},{7,6},{8,9},{9,8},{10,11... | collective-permute-start | bytes 3145736 | tf_op jit(solution)/shard_map/ppermute | solution.py:10
  27.2 2.7 collective-permute-start.4
  27.7 9.4 %collective-permute-start = (bf16[3,128]{1,0:T(4,128)(2,1)S(1)}, bf16[3,128]{1,0:T(4,128)(2,1)S(1)}, u32[]{:S(2)}, u32[]{:S(2)}) collective-permute-start(bf16[3,128]{1,0:T(4,128)(2,1)S(1)} %slice.203), channel_id=1, source_target_pairs={{0,1},{1,2},{2,3},{3,4},{4,5},{5,6},{6,7},{7,8},{8,9},{9,10},{10,1... | collective-permute-start | bytes 2312 | tf_op jit(solution)/shard_map/ppermute | solution.py:16
  29.9 3.6 collective-permute-start.6
  33.5 3.6 collective-permute-start.8
  35.4 25.3 %collective-permute-start.5 = (f32[16,128,128]{2,1,0:T(8,128)S(1)}, f32[16,128,128]{2,1,0:T(8,128)S(1)}, u32[]{:S(2)}, u32[]{:S(2)}) collective-permute-start(f32[16,128,128]{2,1,0:T(8,128)S(1)} %add_select_fusion.2), channel_id=1, source_target_pairs={{0,2},{1,3},{2,0},{3,1},{4,6},{5,7},{6,4},{7,5},{8,10},{9,11},{10,... | collective-permute-start | bytes 3145736 | tf_op jit(solution)/shard_map/ppermute | solution.py:10
  37.2 24.4 %copy-start.1 = (f32[1027,2048]{1,0:T(8,128)S(1)}, f32[1027,2048]{1,0:T(8,128)}, u32[]{:S(2)}) copy-start(f32[1027,2048]{1,0:T(8,128)} %copy-done) | copy-start | bytes 25239556
  61.0 24.4 %collective-permute-start.7 = (f32[16,128,128]{2,1,0:T(8,128)S(1)}, f32[16,128,128]{2,1,0:T(8,128)S(1)}, u32[]{:S(2)}, u32[]{:S(2)}) collective-permute-start(f32[16,128,128]{2,1,0:T(8,128)S(1)} %get-tuple-element.425), channel_id=1, source_target_pairs={{0,4},{1,5},{2,6},{3,7},{4,0},{5,1},{6,2},{7,3},{8,12},{9,13},{10,... | collective-permute-start | bytes 3145736 | tf_op jit(solution)/shard_map/ppermute | solution.py:10
  86.9 5.6 %slice-start = ((bf16[15,16,1024]{2,1,0:T(8,128)(2,1)}), bf16[11,16,1024]{2,1,0:T(8,128)(2,1)S(1)}, s32[]{:S(2)}) async-start(bf16[15,16,1024]{2,1,0:T(8,128)(2,1)} %param.15), calls=%async_computation | async-start | bytes 720896 | tf_op jit(solution)/shard_map/slice | solution.py:95
  86.9 207.5 %collective-permute-start.9 = (f32[16,128,128]{2,1,0:T(8,128)}, f32[16,128,128]{2,1,0:T(8,128)}, u32[]{:S(2)}, u32[]{:S(2)}) collective-permute-start(f32[16,128,128]{2,1,0:T(8,128)} %get-tuple-element.427), channel_id=1, source_target_pairs={{0,8},{1,9},{2,10},{3,11},{4,12},{5,13},{6,14},{7,15},{8,0},{9,1},... | collective-permute-start | bytes 3145736 | tf_op jit(solution)/shard_map/ppermute | solution.py:10
  295.9 4.2 slice-start.1
where the time goes:
time: 442 us; the launch traced here: 439 us
  matrix products  217 us (49%)
  other arithmetic  86.5 us (20%)
  local copies, waits for them, and re-layouts  77.5 us (18%)
  waiting for transfers between devices  40 us (9%)
  starting transfers between devices  16.2 us (4%)
    dot_general x16, matrix products, near_part(): return jnp.dot(near_weight, own_values, preferred_element_type=jnp.float32)  201 us
    convert_element_type x16, other arithmetic, far_part(): far_query = (query_float[:, None, :] * far_scale.T[:, :, None]).astype(jn...  62.1 us
    ppermute x7, waiting for transfers between devices, partner(): lax.ppermute(x, axis, [(i, i ^ 1 << distance) for i in range(lax.axis_siz...  40 us
    dynamic_slice x32, local copies, waits for them, and re-layouts, far_step(): lax.dynamic_slice_in_dim(near_all, head_idx * head_width, head_width, 1)  20.3 us
    dynamic_slice x16, local copies, waits for them, and re-layouts, far_part(): lax.dynamic_index_in_dim(buckets, head_idx, 1, keepdims=False)  14.8 us
    dynamic_update_slice x32, local copies, waits for them, and re-layouts, finish(): lax.dynamic_update_slice_in_dim(output, normed.astype(jnp.bfloat16), head...  14.3 us
    dynamic_slice x16, local copies, waits for them, and re-layouts, finish(): lax.dynamic_slice_in_dim(norm_gain, head_idx * head_width, head_width, 0)  12.3 us
    ppermute x3, starting transfers between devices, from_behind(): return lax.ppermute(x, axis, pairs)  9.03 us
  transfers between devices with their start and end apart: 10, of which 4 were waited for; matrix products, arithmetic and copies ran while one was open for 51% of the time, Pallas kernels for 0%

commit v1 on v0

v1 whole, which is shorter than its diff:
```python
import functools

import jax
import jax.numpy as jnp
from jax import lax
from jax.experimental import pallas as pl
from jax.experimental.pallas import tpu as pltpu
from jax.sharding import PartitionSpec as P

EPSILON = 1e-05
TILE = 128
SUB = 8
GROUP = 2
BF16 = jnp.bfloat16
F32 = jnp.float32
VMEM_BYTES = 40 * 1024 * 1024


def bits_of(number):
    return number.bit_length() - 1


def dot(a, b):
    return jnp.dot(a, b, preferred_element_type=F32)


def scaled(x, row):
    return x * row.astype(BF16)


def conv_tile(padded, weight, row, column, width):
    taps = weight.shape[0]
    first = SUB - taps + 1 + row
    total = None
    for tap in range(taps):
        term = padded[first + tap : first + tap + TILE, column : column + width] * weight[
            tap : tap + 1, column : column + width
        ]
        total = term if total is None else total + term
    half = total * 0.5
    return half + half * jnp.tanh(half)


def fill(padded, rim, current, column):
    rows, width = current.shape
    rim_rows = rim.shape[0]
    padded[SUB - rim_rows : SUB, column : column + width] = rim.astype(F32)
    padded[SUB : SUB + rows, column : column + width] = current.astype(F32)


def spread(cumul, places, width):
    heads = cumul.shape[0]
    return jnp.concatenate(
        [jnp.broadcast_to(cumul[:, at : at + 1], (heads, width)) for at in places], axis=1
    )


def tables(decay, level_weight, table, length, near_count):
    def put(index, value):
        for head in range(value.shape[0]):
            table[head, index : index + 1, :] = value[head : head + 1, :]

    lane = lax.broadcasted_iota(jnp.int32, decay.shape, 1)
    cumul = decay
    step = 1
    while step < length:
        cumul = cumul + jnp.where(lane >= step, pltpu.roll(cumul, step, 1), 0.0)
        step *= 2
    centre = spread(cumul, [at + TILE // 2 for at in range(0, length, TILE)], TILE)
    rise = jnp.exp(cumul - centre)
    put(0, jnp.exp(centre - cumul))
    tile_bits = bits_of(TILE)
    for level in range(tile_bits + 1):
        put(1 + level, level_weight[level].astype(F32) * rise)
    for level in range(tile_bits + 1, near_count):
        half = 1 << (level - 1)
        edge = spread(cumul, [at + half - 1 for at in range(0, length, 2 * half)], 2 * half)
        gap = cumul - edge
        upper = (lane & half) != 0
        fade = jnp.exp(jnp.where(upper, gap, -gap))
        put(1 + level, jnp.where(upper, level_weight[level].astype(F32), 1.0) * fade)
    fall = jnp.exp(cumul)
    for level in range(near_count, level_weight.shape[0]):
        put(1 + level, level_weight[level].astype(F32) * fall)
    put(1 + level_weight.shape[0], jnp.exp(cumul[:, length - 1 :] - cumul))


def prepare_kernel(
    near_count,
    query_in,
    key_in,
    value_in,
    rim_first,
    rim,
    weight_first,
    weight,
    decay,
    level_weight,
    query_turned,
    key_out,
    value_turned,
    table,
    state,
    padded,
):
    step = pl.program_id(0)
    length = query_in.shape[0]
    width = query_in.shape[1]
    group = state.shape[0]

    @pl.when(step == 0)
    def _():
        tables(decay[...], level_weight, table, length, near_count)
        fill(padded, rim_first[:, :width], query_in[...], 0)
        fill(padded, rim_first[:, width:], key_in[...], width)
        for row in range(0, length, TILE):
            query_tile = conv_tile(padded, weight_first, row, 0, width)
            query_turned[:, row : row + TILE] = query_tile.T.astype(BF16)
            key_tile = conv_tile(padded, weight_first, row, width, width)
            key_out[row : row + TILE, :] = key_tile.astype(BF16)

    fill(padded, rim[...], value_in[...], 0)
    tail_at = level_weight.shape[0] + 1
    head_width = state.shape[1]
    for own in range(group):
        at = own * head_width
        for row in range(0, length, TILE):
            tile = conv_tile(padded, weight, row, at, head_width)
            value_turned[at : at + head_width, row : row + TILE] = tile.T.astype(BF16)
        tail = table[step * group + own, tail_at : tail_at + 1, :]
        state[own] = dot(scaled(value_turned[at : at + head_width, :], tail), key_out[...])


def near_kernel(
    near_count, query_turned, key, value_turned, table, *rest
):
    near, scores = rest[-2:]
    step = pl.program_id(0)
    length = key.shape[0]
    tile_bits = bits_of(TILE)
    sub_bits = bits_of(SUB)

    @pl.when(step == 0)
    def _():
        for at in range(0, length, TILE):
            scores[at : at + TILE, :] = dot(
                key[at : at + TILE, :], query_turned[:, at : at + TILE]
            )

    def row_of(index, start, size):
        return table[0, index : index + 1, start : start + size]

    mid_states = {}
    for level in range(tile_bits + 1, near_count):
        half = 1 << (level - 1)
        for start in range(0, length, 2 * half):
            faded = scaled(value_turned[:, start : start + half], row_of(1 + level, start, half))
            mid_states[level, start] = dot(faded, key[start : start + half, :]).astype(BF16)

    sub_row = lax.broadcasted_iota(jnp.int32, (SUB, TILE), 0)
    sub_lane = lax.broadcasted_iota(jnp.int32, (SUB, TILE), 1)
    inner = sub_lane & (SUB - 1)
    inner_differ = inner ^ sub_row
    inner_causal = inner >= sub_row
    tile_of_lane = sub_lane >> sub_bits
    counts = TILE // SUB
    outer_row = lax.broadcasted_iota(jnp.int32, (counts, TILE), 0)
    outer = lax.broadcasted_iota(jnp.int32, (counts, TILE), 1) >> sub_bits
    outer_differ = outer ^ outer_row
    outer_causal = outer > outer_row

    for at in range(0, length, TILE):
        diagonal = jnp.broadcast_to(row_of(1, at, TILE), (SUB, TILE))
        for level in range(1, sub_bits + 1):
            diagonal = jnp.where(
                inner_differ >= 1 << (level - 1), row_of(1 + level, at, TILE), diagonal
            )
        diagonal = jnp.where(inner_causal, diagonal, 0.0)
        beside = jnp.broadcast_to(row_of(2 + sub_bits, at, TILE), (counts, TILE))
        for level in range(sub_bits + 2, tile_bits + 1):
            beside = jnp.where(
                outer_differ >= 1 << (level - sub_bits - 1), row_of(1 + level, at, TILE), beside
            )
        beside = jnp.where(outer_causal, beside, 0.0)
        mixing = jnp.concatenate(
            [
                jnp.where(
                    tile_of_lane == tile,
                    diagonal,
                    jnp.broadcast_to(beside[tile : tile + 1, :], (SUB, TILE)),
                )
                for tile in range(counts)
            ],
            axis=0,
        )
        left = [scaled(value_turned[:, at : at + TILE], row_of(0, at, TILE))]
        right = [(scores[at : at + TILE, :] * mixing).astype(BF16)]
        for level in range(tile_bits + 1, near_count):
            half = 1 << (level - 1)
            if at & half:
                left.append(mid_states[level, at // (2 * half) * (2 * half)])
                right.append(
                    scaled(query_turned[:, at : at + TILE], row_of(1 + level, at, TILE))
                )
        near[:, at : at + TILE] = dot(
            jnp.concatenate(left, axis=1), jnp.concatenate(right, axis=0)
        ).astype(BF16)


def far_kernel(near_count, query_turned, table, near, bucket, gain, output):
    length = query_turned.shape[1]
    seq_bits, group, head_width = bucket.shape[:3]
    span = 2 * TILE
    for own in range(group):
        at = own * head_width
        states = jnp.concatenate([bucket[j, own] for j in range(seq_bits)], axis=1)
        for start in range(0, length, span):
            queries = query_turned[:, start : start + span]
            far = jnp.concatenate(
                [
                    scaled(queries, table[own, 1 + near_count + j : 2 + near_count + j, start : start + span])
                    for j in range(seq_bits)
                ],
                axis=0,
            )
            total = dot(states, far) + near[at : at + head_width, start : start + span].astype(F32)
            power = jnp.mean(total * total, axis=0, keepdims=True)
            normed = total * lax.rsqrt(power + EPSILON)
            output[start : start + span, at : at + head_width] = (
                normed.T * gain[:, at : at + head_width]
            ).astype(BF16)


def whole(shape):
    return pl.BlockSpec(shape, lambda i: (0,) * len(shape))


def climb(state, totals, shard_index, seq_bits):
    size = totals.shape[0]
    shards = lax.iota(jnp.int32, size)
    block = state
    buckets = []
    for bit in range(seq_bits):
        pairs = [(i, i ^ 1 << bit) for i in range(size)]
        other = lax.ppermute(block.astype(BF16), "seq", pairs).astype(F32)
        upper = (shard_index >> bit & 1) == 1
        base = shard_index >> bit << bit
        top = (shard_index >> bit | 1) << bit
        before = jnp.logical_and(shards >= base, shards < shard_index)
        in_upper = jnp.logical_and(shards >= top, shards < top + (1 << bit))
        offset = jnp.sum(jnp.where(before[:, None], totals, 0.0), axis=0)
        lift = jnp.where(upper, jnp.exp(offset), 0.0)
        buckets.append((lift[:, None, None] * other).astype(BF16))
        if bit + 1 < seq_bits:
            fade = jnp.exp(jnp.sum(jnp.where(in_upper[:, None], totals, 0.0), axis=0))
            block = (
                jnp.where(upper, 1.0, fade)[:, None, None] * block
                + jnp.where(upper, fade, 1.0)[:, None, None] * other
            )
    return jnp.stack(buckets, axis=0)


def on_device(
    query_inputs, key_inputs, value_inputs, log_decay, level_weight, conv_weight, norm_gain
):
    length, width = query_inputs.shape
    channels = value_inputs.shape[1]
    heads = log_decay.shape[0]
    head_width = channels // heads
    taps = conv_weight.shape[0]
    levels = level_weight.shape[0]
    size = lax.axis_size("seq")
    seq_bits = bits_of(size)
    near_count = levels - seq_bits
    shard_index = lax.axis_index("seq")
    rim = jnp.concatenate(
        [x[length - taps + 1 :] for x in (query_inputs, key_inputs, value_inputs)], axis=1
    )
    rim = lax.ppermute(rim, "seq", [(i, i + 1) for i in range(size - 1)])
    totals = lax.all_gather(jnp.sum(log_decay, axis=1), "seq")

    group_width = GROUP * head_width
    table_count = levels + 2
    params = pltpu.CompilerParams(vmem_limit_bytes=VMEM_BYTES)
    query_turned, key, value_turned, table, state = pl.pallas_call(
        functools.partial(prepare_kernel, near_count),
        grid=(heads // GROUP,),
        in_specs=[
            whole((length, width)),
            whole((length, width)),
            pl.BlockSpec((length, group_width), lambda i: (0, i)),
            pl.BlockSpec((taps - 1, 2 * width), lambda i: (0, 0)),
            pl.BlockSpec((taps - 1, group_width), lambda i: (0, i + 2 * width // group_width)),
            pl.BlockSpec((taps, 2 * width), lambda i: (0, 0)),
            pl.BlockSpec((taps, group_width), lambda i: (0, i + 2 * width // group_width)),
            whole((heads, length)),
            whole((levels, heads, length)),
        ],
        out_specs=[
            whole((width, length)),
            whole((length, width)),
            pl.BlockSpec((group_width, length), lambda i: (i, 0)),
            whole((heads, table_count, length)),
            pl.BlockSpec((GROUP, head_width, width), lambda i: (i, 0, 0)),
        ],
        out_shape=[
            jax.ShapeDtypeStruct((width, length), BF16),
            jax.ShapeDtypeStruct((length, width), BF16),
            jax.ShapeDtypeStruct((channels, length), BF16),
            jax.ShapeDtypeStruct((heads, table_count, length), F32),
            jax.ShapeDtypeStruct((heads, head_width, width), F32),
        ],
        scratch_shapes=[pltpu.VMEM((SUB + length, max(group_width, 2 * width)), F32)],
        compiler_params=params,
        name="prepare",
    )(
        query_inputs,
        key_inputs,
        value_inputs,
        rim,
        rim,
        conv_weight,
        conv_weight,
        log_decay,
        level_weight,
    )

    pieces = min(seq_bits, 4)
    piece_heads = heads // pieces
    near = None
    for piece in range(pieces):
        first = piece * piece_heads
        chained = [] if near is None else [near]
        near = pl.pallas_call(
            functools.partial(near_kernel, near_count),
            grid=(piece_heads,),
            in_specs=[
                whole((width, length)),
                whole((length, width)),
                pl.BlockSpec((head_width, length), lambda i, first=first: (i + first, 0)),
                pl.BlockSpec((1, table_count, length), lambda i, first=first: (i + first, 0, 0)),
            ]
            + [pl.BlockSpec(memory_space=pl.ANY)] * len(chained),
            out_specs=pl.BlockSpec((head_width, length), lambda i, first=first: (i + first, 0)),
            out_shape=jax.ShapeDtypeStruct((channels, length), BF16),
            input_output_aliases={4: 0} if chained else {},
            scratch_shapes=[pltpu.VMEM((length, TILE), F32)],
            compiler_params=params,
            cost_estimate=pl.CostEstimate(
                flops=piece_heads * 2 * length * head_width * 8 * TILE * 4,
                bytes_accessed=4 * piece_heads * head_width * length,
                transcendentals=0,
            ),
            name="near",
        )(query_turned, key, value_turned, table, *chained)

    buckets = climb(state, totals, shard_index, seq_bits)
    return pl.pallas_call(
        functools.partial(far_kernel, near_count),
        grid=(heads // GROUP,),
        in_specs=[
            whole((width, length)),
            pl.BlockSpec((GROUP, table_count, length), lambda i: (i, 0, 0)),
            pl.BlockSpec((group_width, length), lambda i: (i, 0)),
            pl.BlockSpec((seq_bits, GROUP, head_width, width), lambda i: (0, i, 0, 0)),
            pl.BlockSpec((1, group_width), lambda i: (0, i)),
        ],
        out_specs=pl.BlockSpec((length, group_width), lambda i: (0, i)),
        out_shape=jax.ShapeDtypeStruct((length, channels), BF16),
        compiler_params=params,
        name="far",
    )(query_turned, table, near, buckets, norm_gain[None, :])


def solution(mesh):
    return jax.shard_map(
        on_device,
        mesh=mesh,
        in_specs=(
            P(("grp", "seq"), None),
            P(("grp", "seq"), None),
            P(("grp", "seq"), None),
            P(None, ("grp", "seq")),
            P(None, None, ("grp", "seq")),
            P(),
            P(),
        ),
        out_specs=P(("grp", "seq"), None),
        check_vma=False,
    )
```

time: 442 us -> 129 us (0.29)
  matrix products: 217 us -> 0 us
  other arithmetic: 86.5 us -> 7.19 us
  local copies, waits for them, and re-layouts: 77.5 us -> 12.9 us
  blocking collectives: 0 us -> 33.8 us
  Pallas kernels: 0 us -> 26.4 us
  starting transfers between devices: 16.2 us -> 2.57 us
  waiting for transfers between devices: 40 us -> 44.8 us
    dot_general x34 -> x0, matrix products: 217 us -> none  [the longest x16 201 us: near_part(): return jnp.dot(near_weight, own_values, preferred_element_type=jnp.float32)]
    convert_element_type x70 -> x2, other arithmetic: 76.3 us -> 2.31 us  [climb(): other = lax.ppermute(block.astype(BF16), 'seq', pairs).astype(F32)]
    dynamic_slice x80 -> x0, local copies, waits for them, and re-layouts: 47.6 us -> none  [the longest x32 20.3 us: far_step(): lax.dynamic_slice_in_dim(near_all, head_idx * head_width, head_width, 1)]
    unnamed x0 -> x1, blocking collectives: none -> 33.8 us
    pallas_call x0 -> x6, Pallas kernels: none -> 26.4 us  [the longest x1 11 us: on_device(): pl.pallas_call(functools.partial(prepare_kernel, near_count), grid=(heads...]
    dynamic_update_slice x32 -> x0, local copies, waits for them, and re-layouts: 14.3 us -> none  [finish(): lax.dynamic_update_slice_in_dim(output, normed.astype(jnp.bfloat16), head...]
    ppermute x10 -> x5, starting transfers between devices: 16.2 us -> 2.57 us  [the longest x1 2.36 us: on_device(): rim = lax.ppermute(rim, 'seq', [(i, i + 1) for i in range(size - 1)])]
    unnamed x8 -> x21, local copies, waits for them, and re-layouts: 0.89 us -> 10.6 us
  transfers between devices with their start and end apart: 10 -> 5, of which waited for: 4 -> 4; matrix products, arithmetic and copies ran while one was open for 51% -> 2% of each run, Pallas kernels for 0% -> 7%
where the time goes in v1:
time: 129 us
  waiting for transfers between devices  44.8 us (35%)
  blocking collectives  33.8 us (26%)
  Pallas kernels  26.4 us (20%)
  local copies, waits for them, and re-layouts  12.9 us (10%)
  other arithmetic  7.19 us (6%)
  starting transfers between devices  2.57 us (2%)
    ppermute x4, waiting for transfers between devices, climb(): other = lax.ppermute(block.astype(BF16), 'seq', pairs).astype(F32)  44.8 us
    unnamed x1, blocking collectives  33.8 us
    pallas_call x1, Pallas kernels, on_device(): pl.pallas_call(functools.partial(prepare_kernel, near_count), grid=(heads...  11 us
    unnamed x21, local copies, waits for them, and re-layouts  10.6 us
    pallas_call x4, Pallas kernels, on_device(): pl.pallas_call(functools.partial(near_kernel, near_count), grid=(piece_he...  8.72 us
    pallas_call x1, Pallas kernels, on_device(): pl.pallas_call(functools.partial(far_kernel, near_count), grid=(heads //...  6.69 us
    another operation x4, other arithmetic, climb(): return jnp.stack(buckets, axis=0)  3.71 us
  transfers between devices with their start and end apart: 5, of which 4 were waited for; matrix products, arithmetic and copies ran while one was open for 2% of the time, Pallas kernels for 7%

profile of v1, /device:TPU:0, one launch (start us, length us, event | category | flops | bytes accessed | tf_op | source)
XLA Modules:
  0.0 128.6 jit_solution(2001471641314214313)
XLA Ops:
  0.0 0.8 slice.11
  0.8 0.7 slice.10
  1.5 0.7 slice.9
  2.2 2.4 %collective-permute-start = (bf16[3,2304]{1,0:T(4,128)(2,1)S(1)}, bf16[3,2304]{1,0:T(4,128)(2,1)S(1)}, u32[]{:S(2)}, u32[]{:S(2)}) collective-permute-start(bf16[3,2304]{1,0:T(4,128)(2,1)S(1)} %pad_maximum_fusion.1), channel_id=1, source_target_pairs={{0,1},{1,2},{2,3},{3,4},{4,5},{5,6},{6,7},{7,8},{8,9},{9,10},{10,1... | collective-permute-start | bytes 41480 | tf_op jit(solution)/shard_map/ppermute | solution.py:279
  4.5 1.0 reduce_sum.72
  5.5 1.2 dynamic-slice
  7.4 0.2 dynamic-update-slice
  7.6 33.8 %all-reduce = f32[256]{0:T(256)S(1)} all-reduce(f32[256]{0:T(256)S(1)} %dynamic-update-slice), channel_id=2, replica_groups=mesh['grp'=2,'seq'=16] {'seq'}, use_global_device_ids=true, to_apply=%add | all-reduce | flops 256 | bytes 2048
  41.5 0.1 reshape.83
  41.6 0.1 select_reduce_fusion.6
  41.7 0.0 collective-permute-done.rim_first.rim
  41.8 0.0 copy-start
  41.8 2.2 %copy-done = bf16[1024,2048]{1,0:T(8,128)(2,1)S(1)} copy-done((bf16[1024,2048]{1,0:T(8,128)(2,1)S(1)}, bf16[1024,2048]{1,0:T(8,128)(2,1)}, u32[]{:S(2)}) %copy-start) | copy-done | bytes 4194328
  43.9 0.0 copy-start.1
  44.0 1.0 copy-done.1
  45.0 0.0 copy-start.2
  45.0 0.9 copy-done.2
  45.9 0.0 copy-start.3
  45.9 0.9 copy-done.3
  46.9 0.0 copy-start.4
  46.9 0.8 copy-done.4
  47.7 0.0 copy-start.5
  47.7 0.8 copy-done.5
  48.5 11.0 %prepare.1 = (bf16[128,1024]{1,0:T(8,128)(2,1)S(1)}, bf16[1024,128]{1,0:T(8,128)(2,1)S(1)}, bf16[2048,1024]{1,0:T(8,128)(2,1)S(1)}, f32[16,17,1024]{2,1,0:T(8,128)S(1)}, f32[16,128,128]{2,1,0:T(8,128)S(1)}) custom-call(bf16[1024,128]{1,0:T(8,128)(2,1)S(1)} %copy-done.2, bf16[1024,128]{1,0:T(8,128)(2,1)S(1)} %copy-done.3, bf16[1024,2048]{1,0:T(8,128)(2,1)S(1)} %copy-done, ...), custom_call_target="tpu_custom_call" | custom-call | tf_op jit(solution)/shard_map/prepare/pallas_call | solution.py:285
  59.4 0.0 copy-start.7
  59.5 2.0 %copy-done.7 = bf16[2048,1024]{1,0:T(8,128)(2,1)} copy-done((bf16[2048,1024]{1,0:T(8,128)(2,1)}, bf16[2048,1024]{1,0:T(8,128)(2,1)S(1)}, u32[]{:S(2)}) %copy-start.7) | copy-done | bytes 4194328
  61.5 0.9 convert_element_type.36
  62.3 0.0 collective-permute-start.1
  62.4 2.2 %collective-permute-done.1 = bf16[16,128,128]{2,1,0:T(8,128)(2,1)} collective-permute-done((bf16[16,128,128]{2,1,0:T(8,128)(2,1)}, bf16[16,128,128]{2,1,0:T(8,128)(2,1)}, u32[]{:S(2)}, u32[]{:S(2)}) %collective-permute-start.1) | collective-permute-done | bytes 524320 | tf_op jit(solution)/shard_map/ppermute | solution.py:245
  64.6 1.4 %fusion.12 = bf16[16,128,128]{2,1,0:T(8,128)(2,1)S(1)} fusion(bf16[16,128,128]{2,1,0:T(8,128)(2,1)} %collective-permute-done.1, f32[16]{0:T(128)S(1)} %get-tuple-element.32, f32[16,128,128]{2,1,0:T(8,128)S(1)} %get-tuple-element.14, f32[16]{0:T(128)S(1)} %get-tuple-element.31), kind=kLoop, calls=%fused_computation.46 | loop fusion | flops 1310720 | bytes 2097280 | tf_op jit(solution)/shard_map/convert_element_type | solution.py:245
  66.0 0.1 collective-permute-start.2
  66.2 13.9 %collective-permute-done.2 = bf16[16,128,128]{2,1,0:T(8,128)(2,1)S(1)} collective-permute-done((bf16[16,128,128]{2,1,0:T(8,128)(2,1)S(1)}, bf16[16,128,128]{2,1,0:T(8,128)(2,1)S(1)}, u32[]{:S(2)}, u32[]{:S(2)}) %collective-permute-start.2) | collective-permute-done | bytes 524320 | tf_op jit(solution)/shard_map/ppermute | solution.py:245
  80.1 1.6 %fusion.11 = (bf16[1,16,128,128]{3,2,1,0:T(8,128)(2,1)S(1)}, bf16[16,128,128]{2,1,0:T(8,128)(2,1)S(1)}, bf16[1,16,128,128]{3,2,1,0:T(8,128)(2,1)S(1)}) fusion(bf16[16,128,128]{2,1,0:T(8,128)(2,1)} %collective-permute-done.1, f32[16]{0:T(128)S(1)} %broadcast_select_fusion.9, bf16[16,128,128]{2,1,0:T(8,128)(2,1)S(1)} %collective-permute-done.2, ...), kind=kLoop, calls=%fused_computation.19 | loop fusion | flops 3407872 | bytes 3670400 | tf_op jit(solution)/shard_map/stack | solution.py:260
  81.7 0.1 collective-permute-start.3
  81.8 0.0 copy-done.8
  81.8 2.2 %near.4.rest_0_ = bf16[2048,1024]{1,0:T(8,128)(2,1)S(1)} custom-call(bf16[128,1024]{1,0:T(8,128)(2,1)S(1)} %get-tuple-element.10.query_turned, bf16[1024,128]{1,0:T(8,128)(2,1)S(1)} %get-tuple-element.12.key, bf16[2048,1024]{1,0:T(8,128)(2,1)S(1)} %copy-done.8, f32[16,17,1024]{2,1,0:T(8,128)S(1)} %get-tuple-element.11.table), custom_call_target="tpu_custom_call" | custom-call | flops 4294967296 | bytes 2097152 | tf_op jit(solution)/shard_map/near/pallas_call | solution.py:334
  84.0 2.2 %near.5.rest_0_ = bf16[2048,1024]{1,0:T(8,128)(2,1)S(1)} custom-call(bf16[128,1024]{1,0:T(8,128)(2,1)S(1)} %get-tuple-element.10.query_turned, bf16[1024,128]{1,0:T(8,128)(2,1)S(1)} %get-tuple-element.12.key, bf16[2048,1024]{1,0:T(8,128)(2,1)S(1)} %copy-done.8, f32[16,17,1024]{2,1,0:T(8,128)S(1)} %get-tuple-element.11.table, ...), custom_call_target="tpu_custom_call", output_to_operand_aliasing={{}: (4, {})} | custom-call | flops 4294967296 | bytes 2097152 | tf_op jit(solution)/shard_map/near/pallas_call | solution.py:334
  86.2 8.7 %collective-permute-done.3 = bf16[16,128,128]{2,1,0:T(8,128)(2,1)S(1)} collective-permute-done((bf16[16,128,128]{2,1,0:T(8,128)(2,1)S(1)}, bf16[16,128,128]{2,1,0:T(8,128)(2,1)S(1)}, u32[]{:S(2)}, u32[]{:S(2)}) %collective-permute-start.3) | collective-permute-done | bytes 524320 | tf_op jit(solution)/shard_map/ppermute | solution.py:245
  94.9 1.7 %fusion.9 = (bf16[1,16,128,128]{3,2,1,0:T(8,128)(2,1)S(1)}, bf16[16,128,128]{2,1,0:T(8,128)(2,1)S(1)}) fusion(bf16[16,128,128]{2,1,0:T(8,128)(2,1)S(1)} %collective-permute-done.3, f32[16]{0:T(128)S(1)} %broadcast_select_fusion.3, f32[16]{0:T(128)S(1)} %get-tuple-element.28, bf16[16,128,128]{2,1,0:T(8,128)(2,1)S(1)} %collective-permute-done.2, ...), kind=kLoop, calls=%fused_computation.17 | loop fusion | flops 3932160 | bytes 3670464 | tf_op jit(solution)/shard_map/stack | solution.py:260
  96.6 0.1 collective-permute-start.4
  96.6 2.2 %near.6.rest_0_ = bf16[2048,1024]{1,0:T(8,128)(2,1)S(1)} custom-call(bf16[128,1024]{1,0:T(8,128)(2,1)S(1)} %get-tuple-element.10.query_turned, bf16[1024,128]{1,0:T(8,128)(2,1)S(1)} %get-tuple-element.12.key, bf16[2048,1024]{1,0:T(8,128)(2,1)S(1)} %copy-done.8, f32[16,17,1024]{2,1,0:T(8,128)S(1)} %get-tuple-element.11.table, ...), custom_call_target="tpu_custom_call", output_to_operand_aliasing={{}: (4, {})} | custom-call | flops 4294967296 | bytes 2097152 | tf_op jit(solution)/shard_map/near/pallas_call | solution.py:334
  98.8 2.2 %near.7 = bf16[2048,1024]{1,0:T(8,128)(2,1)S(1)} custom-call(bf16[128,1024]{1,0:T(8,128)(2,1)S(1)} %get-tuple-element.10.query_turned, bf16[1024,128]{1,0:T(8,128)(2,1)S(1)} %get-tuple-element.12.key, bf16[2048,1024]{1,0:T(8,128)(2,1)S(1)} %copy-done.8, f32[16,17,1024]{2,1,0:T(8,128)S(1)} %get-tuple-element.11.table, ...), custom_call_target="tpu_custom_call", output_to_operand_aliasing={{}: (4, {})} | custom-call | flops 4294967296 | bytes 2097152 | tf_op jit(solution)/shard_map/near/pallas_call | solution.py:334
  101.0 20.0 %collective-permute-done.4 = bf16[16,128,128]{2,1,0:T(8,128)(2,1)S(1)} collective-permute-done((bf16[16,128,128]{2,1,0:T(8,128)(2,1)S(1)}, bf16[16,128,128]{2,1,0:T(8,128)(2,1)S(1)}, u32[]{:S(2)}, u32[]{:S(2)}) %collective-permute-start.4) | collective-permute-done | bytes 524320 | tf_op jit(solution)/shard_map/ppermute | solution.py:245
  121.0 0.2 fusion.8
  121.2 0.0 copy-start.6
  121.2 0.3 pad_maximum_fusion.bucket
  121.4 0.4 copy-done.6
  121.9 6.7 %far.1 = bf16[1024,2048]{1,0:T(8,128)(2,1)} custom-call(bf16[128,1024]{1,0:T(8,128)(2,1)S(1)} %get-tuple-element.10.query_turned, f32[16,17,1024]{2,1,0:T(8,128)S(1)} %get-tuple-element.11.table, bf16[2048,1024]{1,0:T(8,128)(2,1)S(1)} %near.7, bf16[4,16,128,128]{3,2,1,0:T(8,128)(2,1)S(1)} %pad_maximum_fusion.bucket, f32[1,2048]{1,0:T(1,128)S(1)} %bitcast.10), custom_call_target="tpu_custom_call" | custom-call | tf_op jit(solution)/shard_map/far/pallas_call | solution.py:358
  (14 shorter events, 0.1 us)
Async XLA Ops:
  2.2 39.6 %collective-permute-start = (bf16[3,2304]{1,0:T(4,128)(2,1)S(1)}, bf16[3,2304]{1,0:T(4,128)(2,1)S(1)}, u32[]{:S(2)}, u32[]{:S(2)}) collective-permute-start(bf16[3,2304]{1,0:T(4,128)(2,1)S(1)} %pad_maximum_fusion.1), channel_id=1, source_target_pairs={{0,1},{1,2},{2,3},{3,4},{4,5},{5,6},{6,7},{7,8},{8,9},{9,10},{10,1... | collective-permute-start | bytes 41480 | tf_op jit(solution)/shard_map/ppermute | solution.py:279
  41.8 2.2 %copy-start = (bf16[1024,2048]{1,0:T(8,128)(2,1)S(1)}, bf16[1024,2048]{1,0:T(8,128)(2,1)}, u32[]{:S(2)}) copy-start(bf16[1024,2048]{1,0:T(8,128)(2,1)} %value_in.1) | copy-start | bytes 12582916
  43.9 1.0 copy-start.1
  45.0 0.9 copy-start.2
  45.9 0.9 copy-start.3
  46.9 0.8 copy-start.4
  47.7 0.8 copy-start.5
  59.4 2.0 %copy-start.7 = (bf16[2048,1024]{1,0:T(8,128)(2,1)}, bf16[2048,1024]{1,0:T(8,128)(2,1)S(1)}, u32[]{:S(2)}) copy-start(bf16[2048,1024]{1,0:T(8,128)(2,1)S(1)} %get-tuple-element.13.value_turned) | copy-start | bytes 12582916
  62.3 2.3 %collective-permute-start.1 = (bf16[16,128,128]{2,1,0:T(8,128)(2,1)}, bf16[16,128,128]{2,1,0:T(8,128)(2,1)}, u32[]{:S(2)}, u32[]{:S(2)}) collective-permute-start(bf16[16,128,128]{2,1,0:T(8,128)(2,1)} %convert_element_type.36), channel_id=1, source_target_pairs={{0,1},{1,0},{2,3},{3,2},{4,5},{5,4},{6,7},{7,6},{8,9},{9,8},{10,11... | collective-permute-start | bytes 1572872 | tf_op jit(solution)/shard_map/ppermute | solution.py:245
  64.6 17.2 %copy-start.8 = (bf16[2048,1024]{1,0:T(8,128)(2,1)S(1)}, bf16[2048,1024]{1,0:T(8,128)(2,1)}, u32[]{:S(2)}) copy-start(bf16[2048,1024]{1,0:T(8,128)(2,1)} %copy-done.7) | copy-start | bytes 12582916
  66.0 14.0 %collective-permute-start.2 = (bf16[16,128,128]{2,1,0:T(8,128)(2,1)S(1)}, bf16[16,128,128]{2,1,0:T(8,128)(2,1)S(1)}, u32[]{:S(2)}, u32[]{:S(2)}) collective-permute-start(bf16[16,128,128]{2,1,0:T(8,128)(2,1)S(1)} %fusion.12), channel_id=1, source_target_pairs={{0,2},{1,3},{2,0},{3,1},{4,6},{5,7},{6,4},{7,5},{8,10},{9,11},{10,... | collective-permute-start | bytes 1572872 | tf_op jit(solution)/shard_map/ppermute | solution.py:245
  81.7 13.2 %collective-permute-start.3 = (bf16[16,128,128]{2,1,0:T(8,128)(2,1)S(1)}, bf16[16,128,128]{2,1,0:T(8,128)(2,1)S(1)}, u32[]{:S(2)}, u32[]{:S(2)}) collective-permute-start(bf16[16,128,128]{2,1,0:T(8,128)(2,1)S(1)} %get-tuple-element.23), channel_id=1, source_target_pairs={{0,4},{1,5},{2,6},{3,7},{4,0},{5,1},{6,2},{7,3},{8,12},{9,13},{10,... | collective-permute-start | bytes 1572872 | tf_op jit(solution)/shard_map/ppermute | solution.py:245
  96.6 24.4 %collective-permute-start.4 = (bf16[16,128,128]{2,1,0:T(8,128)(2,1)S(1)}, bf16[16,128,128]{2,1,0:T(8,128)(2,1)S(1)}, u32[]{:S(2)}, u32[]{:S(2)}) collective-permute-start(bf16[16,128,128]{2,1,0:T(8,128)(2,1)S(1)} %get-tuple-element.26), channel_id=1, source_target_pairs={{0,8},{1,9},{2,10},{3,11},{4,12},{5,13},{6,14},{7,15},{8,0},{9,1},... | collective-permute-start | bytes 1572872 | tf_op jit(solution)/shard_map/ppermute | solution.py:245
  121.2 0.7 copy-start.6

commit v2 on v1

--- a/solution.py
+++ b/solution.py
@@ -13,7 +13,7 @@
 GROUP = 2
 BF16 = jnp.bfloat16
 F32 = jnp.float32
-VMEM_BYTES = 40 * 1024 * 1024
+MIB = 1024 * 1024
 
 
 def bits_of(number):
@@ -207,18 +207,32 @@
         ).astype(BF16)
 
 
-def far_kernel(near_count, query_turned, table, near, bucket, gain, output):
+def far_kernel(near_count, query_turned, table, near, gain, digit, lifts, *rest):
+    buckets, output = rest[:-1], rest[-1]
     length = query_turned.shape[1]
-    seq_bits, group, head_width = bucket.shape[:3]
+    group, head_width = buckets[0].shape[:2]
+    seq_bits = (len(buckets) + 1) // 2
+    upper = digit[0] == 1
     span = 2 * TILE
     for own in range(group):
         at = own * head_width
-        states = jnp.concatenate([bucket[j, own] for j in range(seq_bits)], axis=1)
+        parts = [buckets[0][own]]
+        for j in range(1, seq_bits):
+            mine, other = buckets[2 * j - 1][own], buckets[2 * j][own]
+            first = jnp.where(upper, other, mine)
+            second = jnp.where(upper, mine, other)
+            parts.append(jnp.concatenate([first, second], axis=0))
+        states = jnp.concatenate(parts, axis=1)
+        head = pl.program_id(0) * group + own
+        far_rows = [
+            table[own, 1 + near_count + j : 2 + near_count + j, :] * lifts[j, head]
+            for j in range(seq_bits)
+        ]
         for start in range(0, length, span):
             queries = query_turned[:, start : start + span]
             far = jnp.concatenate(
                 [
-                    scaled(queries, table[own, 1 + near_count + j : 2 + near_count + j, start : start + span])
+                    scaled(queries, far_rows[j][:, start : start + span])
                     for j in range(seq_bits)
                 ],
                 axis=0,
@@ -235,29 +249,45 @@
     return pl.BlockSpec(shape, lambda i: (0,) * len(shape))
 
 
-def climb(state, totals, shard_index, seq_bits):
-    size = totals.shape[0]
-    shards = lax.iota(jnp.int32, size)
+def exchange(x, bit):
+    size = lax.axis_size("seq")
+    return lax.ppermute(x, "seq", [(i, i ^ 1 << bit) for i in range(size)])
+
+
+def climb(state, total, shard_index, seq_bits):
     block = state
+    block_total = total
+    offset = jnp.zeros_like(total)
+    lifts = []
     buckets = []
     for bit in range(seq_bits):
-        pairs = [(i, i ^ 1 << bit) for i in range(size)]
-        other = lax.ppermute(block.astype(BF16), "seq", pairs).astype(F32)
-        upper = (shard_index >> bit & 1) == 1
-        base = shard_index >> bit << bit
-        top = (shard_index >> bit | 1) << bit
-        before = jnp.logical_and(shards >= base, shards < shard_index)
-        in_upper = jnp.logical_and(shards >= top, shards < top + (1 << bit))
-        offset = jnp.sum(jnp.where(before[:, None], totals, 0.0), axis=0)
-        lift = jnp.where(upper, jnp.exp(offset), 0.0)
-        buckets.append((lift[:, None, None] * other).astype(BF16))
+        other = exchange(block.astype(BF16), bit)
+        other_total = exchange(block_total, bit)
+        digit = shard_index >> bit & 1
+        upper = digit == 1
+        lifts.append(jnp.where(upper, jnp.exp(offset), 0.0))
+        buckets.append(other)
         if bit + 1 < seq_bits:
-            fade = jnp.exp(jnp.sum(jnp.where(in_upper[:, None], totals, 0.0), axis=0))
-            block = (
-                jnp.where(upper, 1.0, fade)[:, None, None] * block
-                + jnp.where(upper, fade, 1.0)[:, None, None] * other
+            share = block.shape[1] // 2
+            own_part = lax.dynamic_slice_in_dim(block, digit * share, share, 1)
+            other_part = lax.dynamic_slice_in_dim(other, digit * share, share, 1)
+            own_scale = jnp.where(upper, 1.0, jnp.exp(other_total))[:, None, None]
+            other_scale = jnp.where(upper, jnp.exp(block_total), 1.0)[:, None, None]
+            block = own_scale * own_part + other_scale * other_part.astype(F32)
+            block_total = block_total + other_total
+            offset = offset + jnp.where(upper, other_total, 0.0)
+    halves = [buckets[0]]
+    for at in range(1, seq_bits):
+        bucket = buckets[at]
+        for bit in range(at - 1, 0, -1):
+            other = exchange(bucket, bit)
+            bucket = jnp.where(
+                (shard_index >> bit & 1) == 1,
+                jnp.concatenate([other, bucket], axis=1),
+                jnp.concatenate([bucket, other], axis=1),
             )
-    return jnp.stack(buckets, axis=0)
+        halves += [bucket, exchange(bucket, 0)]
+    return jnp.stack(lifts), halves
 
 
 def on_device(
@@ -277,11 +307,11 @@
         [x[length - taps + 1 :] for x in (query_inputs, key_inputs, value_inputs)], axis=1
     )
     rim = lax.ppermute(rim, "seq", [(i, i + 1) for i in range(size - 1)])
-    totals = lax.all_gather(jnp.sum(log_decay, axis=1), "seq")
+    total = jnp.sum(log_decay, axis=1)
 
     group_width = GROUP * head_width
     table_count = levels + 2
-    params = pltpu.CompilerParams(vmem_limit_bytes=VMEM_BYTES)
+    params = pltpu.CompilerParams(vmem_limit_bytes=40 * MIB)
     query_turned, key, value_turned, table, state = pl.pallas_call(
         functools.partial(prepare_kernel, near_count),
         grid=(heads // GROUP,),
@@ -311,7 +341,7 @@
             jax.ShapeDtypeStruct((heads, head_width, width), F32),
         ],
         scratch_shapes=[pltpu.VMEM((SUB + length, max(group_width, 2 * width)), F32)],
-        compiler_params=params,
+        compiler_params=pltpu.CompilerParams(vmem_limit_bytes=60 * MIB),
         name="prepare",
     )(
         query_inputs,
@@ -354,7 +384,8 @@
             name="near",
         )(query_turned, key, value_turned, table, *chained)
 
-    buckets = climb(state, totals, shard_index, seq_bits)
+    lifts, buckets = climb(state, total, shard_index, seq_bits)
+    digit = (shard_index & 1).astype(jnp.int32).reshape(1)
     return pl.pallas_call(
         functools.partial(far_kernel, near_count),
         grid=(heads // GROUP,),
@@ -362,14 +393,16 @@
             whole((width, length)),
             pl.BlockSpec((GROUP, table_count, length), lambda i: (i, 0, 0)),
             pl.BlockSpec((group_width, length), lambda i: (i, 0)),
-            pl.BlockSpec((seq_bits, GROUP, head_width, width), lambda i: (0, i, 0, 0)),
             pl.BlockSpec((1, group_width), lambda i: (0, i)),
-        ],
+            pl.BlockSpec(memory_space=pltpu.SMEM),
+            pl.BlockSpec(memory_space=pltpu.SMEM),
+        ]
+        + [pl.BlockSpec((GROUP,) + x.shape[1:], lambda i: (i, 0, 0)) for x in buckets],
         out_specs=pl.BlockSpec((length, group_width), lambda i: (0, i)),
         out_shape=jax.ShapeDtypeStruct((length, channels), BF16),
         compiler_params=params,
         name="far",
-    )(query_turned, table, near, buckets, norm_gain[None, :])
+    )(query_turned, table, near, norm_gain[None, :], digit, lifts, *buckets)
 
 
 def solution(mesh):

time: 129 us -> 70.9 us (0.55)
  blocking collectives: 33.8 us -> 0 us
  waiting for transfers between devices: 44.8 us -> 12.5 us
  starting transfers between devices: 2.57 us -> 19.1 us
  local copies, waits for them, and re-layouts: 12.9 us -> 4.99 us
  other arithmetic: 7.19 us -> 4.02 us
  Pallas kernels: 26.4 us -> 29.5 us
    unnamed x1 -> x0, blocking collectives: 33.8 us -> none
    ppermute x4 -> x13, waiting for transfers between devices: 44.8 us -> 11.7 us  [exchange(): return lax.ppermute(x, 'seq', [(i, i ^ 1 << bit) for i in range(size)])]
    ppermute x4 -> x13, starting transfers between devices: 0.22 us -> 16.8 us  [exchange(): return lax.ppermute(x, 'seq', [(i, i ^ 1 << bit) for i in range(size)])]
    unnamed x21 -> x16, local copies, waits for them, and re-layouts: 10.6 us -> 2.81 us
    another operation x4 -> x2, other arithmetic: 3.71 us -> 0.08 us  [climb(): return (jnp.stack(lifts), halves)]
    pallas_call x1, Pallas kernels: 11 us -> 13.2 us  [on_device(): pl.pallas_call(functools.partial(prepare_kernel, near_count), grid=(heads...]
    convert_element_type x2 -> x4, other arithmetic: 2.31 us -> 3.56 us  [climb(): other = exchange(block.astype(BF16), bit)]
  transfers between devices with their start and end apart: 5 -> 14, of which waited for: 4 -> 7; matrix products, arithmetic and copies ran while one was open for 2% -> 3% of each run, Pallas kernels for 7% -> 13%
where the time goes in v2:
time: 70.9 us; the launch traced here: 70.4 us
  Pallas kernels  29.5 us (42%)
  starting transfers between devices  19.1 us (27%)
  waiting for transfers between devices  12.5 us (18%)
  local copies, waits for them, and re-layouts  4.99 us (7%)
  other arithmetic  4.02 us (6%)
    ppermute x13, starting transfers between devices, exchange(): return lax.ppermute(x, 'seq', [(i, i ^ 1 << bit) for i in range(size)])  16.8 us
    pallas_call x1, Pallas kernels, on_device(): pl.pallas_call(functools.partial(prepare_kernel, near_count), grid=(heads...  13.2 us
    ppermute x13, waiting for transfers between devices, exchange(): return lax.ppermute(x, 'seq', [(i, i ^ 1 << bit) for i in range(size)])  11.7 us
    pallas_call x4, Pallas kernels, on_device(): pl.pallas_call(functools.partial(near_kernel, near_count), grid=(piece_he...  8.83 us
    pallas_call x1, Pallas kernels, on_device(): pl.pallas_call(functools.partial(far_kernel, near_count), grid=(heads //...  7.4 us
    convert_element_type x4, other arithmetic, climb(): other = exchange(block.astype(BF16), bit)  3.56 us
    unnamed x16, local copies, waits for them, and re-layouts  2.81 us
    ppermute x1, starting transfers between devices, on_device(): rim = lax.ppermute(rim, 'seq', [(i, i + 1) for i in range(size - 1)])  2.36 us
  transfers between devices with their start and end apart: 14, of which 7 were waited for; matrix products, arithmetic and copies ran while one was open for 3% of the time, Pallas kernels for 13%

profile of v2, /device:TPU:0, one launch (start us, length us, event | category | flops | bytes accessed | tf_op | source)
XLA Modules:
  0.0 70.4 jit_solution(3623971148507727318)
XLA Ops:
  0.0 0.8 %slice.11 = bf16[3,2048]{1,0:T(4,128)(2,1)S(1)} slice(bf16[1024,2048]{1,0:T(8,128)(2,1)} %value_in.1), slice={[1021:1024], [0:2048]} | slice | bytes 24576 | tf_op jit(solution)/shard_map/slice | solution.py:307
  0.8 0.7 slice.10
  1.5 0.7 slice.9
  2.2 2.4 %collective-permute-start = (bf16[3,2304]{1,0:T(4,128)(2,1)S(1)}, bf16[3,2304]{1,0:T(4,128)(2,1)S(1)}, u32[]{:S(2)}, u32[]{:S(2)}) collective-permute-start(bf16[3,2304]{1,0:T(4,128)(2,1)S(1)} %pad_maximum_fusion), channel_id=1, source_target_pairs={{0,1},{1,2},{2,3},{3,4},{4,5},{5,6},{6,7},{7,8},{8,9},{9,10},{10,1... | collective-permute-start | bytes 41480 | tf_op jit(solution)/shard_map/ppermute | solution.py:309
  4.6 0.8 %collective-permute-done.rim_first.rim = bf16[3,2304]{1,0:T(4,128)(2,1)S(1)} collective-permute-done((bf16[3,2304]{1,0:T(4,128)(2,1)S(1)}, bf16[3,2304]{1,0:T(4,128)(2,1)S(1)}, u32[]{:S(2)}, u32[]{:S(2)}) %collective-permute-start) | collective-permute-done | bytes 13856 | tf_op jit(solution)/shard_map/ppermute | solution.py:309
  5.4 0.6 copy-done.7
  6.0 13.2 %prepare.1 = (bf16[128,1024]{1,0:T(8,128)(2,1)}, bf16[1024,128]{1,0:T(8,128)(2,1)}, bf16[2048,1024]{1,0:T(8,128)(2,1)}, f32[16,17,1024]{2,1,0:T(8,128)}, f32[16,128,128]{2,1,0:T(8,128)}) custom-call(bf16[1024,128]{1,0:T(8,128)(2,1)} %query_in.1, bf16[1024,128]{1,0:T(8,128)(2,1)} %key_in.1, bf16[1024,2048]{1,0:T(8,128)(2,1)} %value_in.1, ...), custom_call_target="tpu_custom_call" | custom-call | tf_op jit(solution)/shard_map/prepare/pallas_call | solution.py:315
  19.3 1.5 %convert_element_type.21 = bf16[16,128,128]{2,1,0:T(8,128)(2,1)S(1)} convert(f32[16,128,128]{2,1,0:T(8,128)} %get-tuple-element.14) | non-fusion elementwise | flops 262144 | bytes 1572864 | tf_op jit(solution)/shard_map/convert_element_type | solution.py:264
  20.7 2.7 %collective-permute-start.4 = (bf16[16,128,128]{2,1,0:T(8,128)(2,1)S(1)}, bf16[16,128,128]{2,1,0:T(8,128)(2,1)S(1)}, u32[]{:S(2)}, u32[]{:S(2)}) collective-permute-start(bf16[16,128,128]{2,1,0:T(8,128)(2,1)S(1)} %convert_element_type.21), channel_id=1, source_target_pairs={{0,1},{1,0},{2,3},{3,2},{4,5},{5,4},{6,7},{7,6},{8,9},{9,8},{10,11... | collective-permute-start | bytes 1572872 | tf_op jit(solution)/shard_map/ppermute | solution.py:254
  23.5 0.1 reduce_sum.9
  23.6 0.1 collective-permute-start.1
  23.7 1.3 %collective-permute-done.1 = f32[16]{0:T(128)S(1)} collective-permute-done((f32[16]{0:T(128)S(1)}, f32[16]{0:T(128)S(1)}, u32[]{:S(2)}, u32[]{:S(2)}) %collective-permute-start.1) | collective-permute-done | bytes 96 | tf_op jit(solution)/shard_map/ppermute | solution.py:254
  25.0 2.6 %collective-permute-start.2 = (f32[16]{0:T(128)S(1)}, f32[16]{0:T(128)S(1)}, u32[]{:S(2)}, u32[]{:S(2)}) collective-permute-start(f32[16]{0:T(128)S(1)} %get-tuple-element.20), channel_id=1, source_target_pairs={{0,2},{1,3},{2,0},{3,1},{4,6},{5,7},{6,4},{7,5},{8,10},{9,11},{10,... | collective-permute-start | bytes 200 | tf_op jit(solution)/shard_map/ppermute | solution.py:254
  27.6 0.0 collective-permute-done.4.rest_0_
  27.6 1.9 %fusion.7 = (bf16[16,64,128]{2,1,0:T(8,128)(2,1)}, f32[16,64,128]{2,1,0:T(8,128)S(1)}) fusion(bf16[16,128,128]{2,1,0:T(8,128)(2,1)S(1)} %collective-permute-done.4.rest_0_, s32[]{:T(128)S(6)} %select_n.113, f32[16]{0:T(128)S(1)} %get-tuple-element.29, f32[16,128,128]{2,1,0:T(8,128)} %get-tuple-element.14, f32[16]{0:T(128)S(1)} %get-tuple-element.28), kind=kLoop, calls=%fused_computation.27 | loop fusion | flops 655360 | bytes 1572996 | tf_op jit(solution)/shard_map/convert_element_type | solution.py:264
  29.5 0.0 collective-permute-start.5
  29.6 0.0 collective-permute-done.2
  29.6 3.0 %collective-permute-start.3 = (f32[16]{0:T(128)S(1)}, f32[16]{0:T(128)S(1)}, u32[]{:S(2)}, u32[]{:S(2)}) collective-permute-start(f32[16]{0:T(128)S(1)} %get-tuple-element.33), channel_id=1, source_target_pairs={{0,4},{1,5},{2,6},{3,7},{4,0},{5,1},{6,2},{7,3},{8,12},{9,13},{10,... | collective-permute-start | bytes 200 | tf_op jit(solution)/shard_map/ppermute | solution.py:254
  32.6 1.5 %collective-permute-done.3 = f32[16]{0:T(128)S(1)} collective-permute-done((f32[16]{0:T(128)S(1)}, f32[16]{0:T(128)S(1)}, u32[]{:S(2)}, u32[]{:S(2)}) %collective-permute-start.3) | collective-permute-done | bytes 96 | tf_op jit(solution)/shard_map/ppermute | solution.py:254
  34.1 3.6 %collective-permute-done.5.rest_1_ = bf16[16,64,128]{2,1,0:T(8,128)(2,1)S(1)} collective-permute-done((bf16[16,64,128]{2,1,0:T(8,128)(2,1)}, bf16[16,64,128]{2,1,0:T(8,128)(2,1)S(1)}, u32[]{:S(2)}, u32[]{:S(2)}) %collective-permute-start.5) | collective-permute-done | bytes 262176 | tf_op jit(solution)/shard_map/ppermute | solution.py:254
  37.7 0.1 fusion.6
  37.9 1.6 %collective-permute-start.7 = (bf16[16,32,128]{2,1,0:T(8,128)(2,1)S(1)}, bf16[16,32,128]{2,1,0:T(8,128)(2,1)S(1)}, u32[]{:S(2)}, u32[]{:S(2)}) collective-permute-start(bf16[16,32,128]{2,1,0:T(8,128)(2,1)S(1)} %get-tuple-element.17), channel_id=1, source_target_pairs={{0,4},{1,5},{2,6},{3,7},{4,0},{5,1},{6,2},{7,3},{8,12},{9,13},{10,... | collective-permute-start | bytes 393224 | tf_op jit(solution)/shard_map/ppermute | solution.py:254
  39.5 0.1 pad_maximum_fusion.1.lifts
  39.6 3.3 %collective-permute-done.7 = bf16[16,32,128]{2,1,0:T(8,128)(2,1)S(1)} collective-permute-done((bf16[16,32,128]{2,1,0:T(8,128)(2,1)S(1)}, bf16[16,32,128]{2,1,0:T(8,128)(2,1)S(1)}, u32[]{:S(2)}, u32[]{:S(2)}) %collective-permute-start.7) | collective-permute-done | bytes 131104 | tf_op jit(solution)/shard_map/ppermute | solution.py:254
  42.9 0.1 add_convert_fusion
  43.0 2.7 %collective-permute-start.10 = (bf16[16,16,128]{2,1,0:T(8,128)(2,1)S(1)}, bf16[16,16,128]{2,1,0:T(8,128)(2,1)S(1)}, u32[]{:S(2)}, u32[]{:S(2)}) collective-permute-start(bf16[16,16,128]{2,1,0:T(8,128)(2,1)S(1)} %add_convert_fusion), channel_id=1, source_target_pairs={{0,8},{1,9},{2,10},{3,11},{4,12},{5,13},{6,14},{7,15},{8,0},{9,1},... | collective-permute-start | bytes 196616 | tf_op jit(solution)/shard_map/ppermute | solution.py:254
  45.7 2.2 %copy-done.3 = bf16[2048,1024]{1,0:T(8,128)(2,1)S(1)} copy-done((bf16[2048,1024]{1,0:T(8,128)(2,1)S(1)}, bf16[2048,1024]{1,0:T(8,128)(2,1)}, u32[]{:S(2)}) %copy-start.3) | copy-done | bytes 4194328
  47.8 2.2 %near.4.rest_0_ = bf16[2048,1024]{1,0:T(8,128)(2,1)S(1)} custom-call(bf16[128,1024]{1,0:T(8,128)(2,1)S(1)} %copy-done.1, bf16[1024,128]{1,0:T(8,128)(2,1)S(1)} %copy-done.5, bf16[2048,1024]{1,0:T(8,128)(2,1)S(1)} %copy-done.3, f32[16,17,1024]{2,1,0:T(8,128)S(1)} %copy-done), custom_call_target="tpu_custom_call" | custom-call | flops 4294967296 | bytes 2097152 | tf_op jit(solution)/shard_map/near/pallas_call | solution.py:364
  50.1 0.0 collective-permute-done.10
  50.1 1.6 %collective-permute-start.11 = (bf16[16,16,128]{2,1,0:T(8,128)(2,1)S(1)}, bf16[16,16,128]{2,1,0:T(8,128)(2,1)S(1)}, u32[]{:S(2)}, u32[]{:S(2)}) collective-permute-start(bf16[16,16,128]{2,1,0:T(8,128)(2,1)S(1)} %collective-permute-done.10), channel_id=1, source_target_pairs={{0,4},{1,5},{2,6},{3,7},{4,0},{5,1},{6,2},{7,3},{8,12},{9,13},{10,... | collective-permute-start | bytes 196616 | tf_op jit(solution)/shard_map/ppermute | solution.py:254
  51.7 2.2 %near.5.rest_0_ = bf16[2048,1024]{1,0:T(8,128)(2,1)S(1)} custom-call(bf16[128,1024]{1,0:T(8,128)(2,1)S(1)} %copy-done.1, bf16[1024,128]{1,0:T(8,128)(2,1)S(1)} %copy-done.5, bf16[2048,1024]{1,0:T(8,128)(2,1)S(1)} %copy-done.3, f32[16,17,1024]{2,1,0:T(8,128)S(1)} %copy-done, bf16[2048,1024]{1,0:T(8,128)(2,1)S(1)} %near.4.rest_0_), custom_call_target="tpu_custom_call", output_to_operand_aliasing={{}: (4, {})} | custom-call | flops 4294967296 | bytes 2097152 | tf_op jit(solution)/shard_map/near/pallas_call | solution.py:364
  53.9 1.5 %collective-permute-start.8 = (bf16[16,32,128]{2,1,0:T(8,128)(2,1)S(1)}, bf16[16,32,128]{2,1,0:T(8,128)(2,1)S(1)}, u32[]{:S(2)}, u32[]{:S(2)}) collective-permute-start(bf16[16,32,128]{2,1,0:T(8,128)(2,1)S(1)} %collective-permute-done.7), channel_id=1, source_target_pairs={{0,2},{1,3},{2,0},{3,1},{4,6},{5,7},{6,4},{7,5},{8,10},{9,11},{10,... | collective-permute-start | bytes 393224 | tf_op jit(solution)/shard_map/ppermute | solution.py:254
  55.4 0.0 collective-permute-done.11
  55.4 0.0 copy-start.4
  55.5 0.7 collective-permute-start.12
  56.1 2.2 %near.6.rest_0_ = bf16[2048,1024]{1,0:T(8,128)(2,1)S(1)} custom-call(bf16[128,1024]{1,0:T(8,128)(2,1)S(1)} %copy-done.1, bf16[1024,128]{1,0:T(8,128)(2,1)S(1)} %copy-done.5, bf16[2048,1024]{1,0:T(8,128)(2,1)S(1)} %copy-done.3, f32[16,17,1024]{2,1,0:T(8,128)S(1)} %copy-done, bf16[2048,1024]{1,0:T(8,128)(2,1)S(1)} %near.5.rest_0_), custom_call_target="tpu_custom_call", output_to_operand_aliasing={{}: (4, {})} | custom-call | flops 4294967296 | bytes 2097152 | tf_op jit(solution)/shard_map/near/pallas_call | solution.py:364
  58.3 0.1 collective-permute-start.6
  58.4 0.5 collective-permute-done.8
  59.0 0.1 maximum_select_fusion.rest_3_
  59.1 0.1 collective-permute-start.9
  59.1 1.3 %collective-permute-done.12 = bf16[16,32,128]{2,1,0:T(8,128)(2,1)S(1)} collective-permute-done((bf16[16,32,128]{2,1,0:T(8,128)(2,1)S(1)}, bf16[16,32,128]{2,1,0:T(8,128)(2,1)S(1)}, u32[]{:S(2)}, u32[]{:S(2)}) %collective-permute-start.12) | collective-permute-done | bytes 131104 | tf_op jit(solution)/shard_map/ppermute | solution.py:254
  60.5 0.1 maximum_select_fusion.1.rest_5_
  60.6 0.0 copy-start.2
  60.6 0.1 collective-permute-start.13
  60.7 2.2 %near.7 = bf16[2048,1024]{1,0:T(8,128)(2,1)S(1)} custom-call(bf16[128,1024]{1,0:T(8,128)(2,1)S(1)} %copy-done.1, bf16[1024,128]{1,0:T(8,128)(2,1)S(1)} %copy-done.5, bf16[2048,1024]{1,0:T(8,128)(2,1)S(1)} %copy-done.4, f32[16,17,1024]{2,1,0:T(8,128)S(1)} %copy-done, bf16[2048,1024]{1,0:T(8,128)(2,1)S(1)} %near.6.rest_0_), custom_call_target="tpu_custom_call", output_to_operand_aliasing={{}: (4, {})} | custom-call | flops 4294967296 | bytes 2097152 | tf_op jit(solution)/shard_map/near/pallas_call | solution.py:364
  62.9 0.0 collective-permute-done.9.rest_4_
  62.9 0.0 collective-permute-done.13.rest_6_
  63.0 7.4 %far.1 = bf16[1024,2048]{1,0:T(8,128)(2,1)} custom-call(bf16[128,1024]{1,0:T(8,128)(2,1)S(1)} %copy-done.1, f32[16,17,1024]{2,1,0:T(8,128)S(1)} %copy-done, bf16[2048,1024]{1,0:T(8,128)(2,1)S(1)} %near.7, f32[1,2048]{1,0:T(1,128)S(1)} %bitcast.9, s32[1]{0:T(128)} %bitcast.1.digit, f32[4,16]{1,0:T(4,128)S(1)} %pad_maximum_fusion.1.lifts, ...), custom_call_target="tpu_custom_call" | custom-call | tf_op jit(solution)/shard_map/far/pallas_call | solution.py:389
  (19 shorter events, 0.1 us)
Async XLA Ops:
  0.0 23.5 %copy-start.6 = (f32[16,1024]{1,0:T(8,128)S(1)}, f32[16,1024]{1,0:T(8,128)}, u32[]{:S(2)}) copy-start(f32[16,1024]{1,0:T(8,128)} %decay.1) | copy-start | bytes 196612
  2.2 3.2 %collective-permute-start = (bf16[3,2304]{1,0:T(4,128)(2,1)S(1)}, bf16[3,2304]{1,0:T(4,128)(2,1)S(1)}, u32[]{:S(2)}, u32[]{:S(2)}) collective-permute-start(bf16[3,2304]{1,0:T(4,128)(2,1)S(1)} %pad_maximum_fusion), channel_id=1, source_target_pairs={{0,1},{1,2},{2,3},{3,4},{4,5},{5,6},{6,7},{7,8},{8,9},{9,10},{10,1... | collective-permute-start | bytes 41480 | tf_op jit(solution)/shard_map/ppermute | solution.py:309
  5.4 0.6 copy-start.7
  19.2 26.4 %copy-start = (f32[16,17,1024]{2,1,0:T(8,128)S(1)}, f32[16,17,1024]{2,1,0:T(8,128)}, u32[]{:S(2)}) copy-start(f32[16,17,1024]{2,1,0:T(8,128)} %get-tuple-element.11.table) | copy-start | bytes 3342340
  19.2 26.4 %copy-start.1 = (bf16[128,1024]{1,0:T(8,128)(2,1)S(1)}, bf16[128,1024]{1,0:T(8,128)(2,1)}, u32[]{:S(2)}) copy-start(bf16[128,1024]{1,0:T(8,128)(2,1)} %get-tuple-element.10.query_turned) | copy-start | bytes 786436
  19.2 26.4 %copy-start.5 = (bf16[1024,128]{1,0:T(8,128)(2,1)S(1)}, bf16[1024,128]{1,0:T(8,128)(2,1)}, u32[]{:S(2)}) copy-start(bf16[1024,128]{1,0:T(8,128)(2,1)} %get-tuple-element.12.key) | copy-start | bytes 786436
  20.7 6.9 %collective-permute-start.4 = (bf16[16,128,128]{2,1,0:T(8,128)(2,1)S(1)}, bf16[16,128,128]{2,1,0:T(8,128)(2,1)S(1)}, u32[]{:S(2)}, u32[]{:S(2)}) collective-permute-start(bf16[16,128,128]{2,1,0:T(8,128)(2,1)S(1)} %convert_element_type.21), channel_id=1, source_target_pairs={{0,1},{1,0},{2,3},{3,2},{4,5},{5,4},{6,7},{7,6},{8,9},{9,8},{10,11... | collective-permute-start | bytes 1572872 | tf_op jit(solution)/shard_map/ppermute | solution.py:254
  23.6 1.4 %collective-permute-start.1 = (f32[16]{0:T(128)S(1)}, f32[16]{0:T(128)S(1)}, u32[]{:S(2)}, u32[]{:S(2)}) collective-permute-start(f32[16]{0:T(128)S(1)} %reduce_sum.9), channel_id=1, source_target_pairs={{0,1},{1,0},{2,3},{3,2},{4,5},{5,4},{6,7},{7,6},{8,9},{9,8},{10,11... | collective-permute-start | bytes 200 | tf_op jit(solution)/shard_map/ppermute | solution.py:254
  25.0 4.5 %collective-permute-start.2 = (f32[16]{0:T(128)S(1)}, f32[16]{0:T(128)S(1)}, u32[]{:S(2)}, u32[]{:S(2)}) collective-permute-start(f32[16]{0:T(128)S(1)} %get-tuple-element.20), channel_id=1, source_target_pairs={{0,2},{1,3},{2,0},{3,1},{4,6},{5,7},{6,4},{7,5},{8,10},{9,11},{10,... | collective-permute-start | bytes 200 | tf_op jit(solution)/shard_map/ppermute | solution.py:254
  29.5 8.2 %collective-permute-start.5 = (bf16[16,64,128]{2,1,0:T(8,128)(2,1)}, bf16[16,64,128]{2,1,0:T(8,128)(2,1)S(1)}, u32[]{:S(2)}, u32[]{:S(2)}) collective-permute-start(bf16[16,64,128]{2,1,0:T(8,128)(2,1)} %get-tuple-element.21), channel_id=1, source_target_pairs={{0,2},{1,3},{2,0},{3,1},{4,6},{5,7},{6,4},{7,5},{8,10},{9,11},{10,... | collective-permute-start | bytes 786440 | tf_op jit(solution)/shard_map/ppermute | solution.py:254
  29.6 4.5 %collective-permute-start.3 = (f32[16]{0:T(128)S(1)}, f32[16]{0:T(128)S(1)}, u32[]{:S(2)}, u32[]{:S(2)}) collective-permute-start(f32[16]{0:T(128)S(1)} %get-tuple-element.33), channel_id=1, source_target_pairs={{0,4},{1,5},{2,6},{3,7},{4,0},{5,1},{6,2},{7,3},{8,12},{9,13},{10,... | collective-permute-start | bytes 200 | tf_op jit(solution)/shard_map/ppermute | solution.py:254
  37.9 5.0 %collective-permute-start.7 = (bf16[16,32,128]{2,1,0:T(8,128)(2,1)S(1)}, bf16[16,32,128]{2,1,0:T(8,128)(2,1)S(1)}, u32[]{:S(2)}, u32[]{:S(2)}) collective-permute-start(bf16[16,32,128]{2,1,0:T(8,128)(2,1)S(1)} %get-tuple-element.17), channel_id=1, source_target_pairs={{0,4},{1,5},{2,6},{3,7},{4,0},{5,1},{6,2},{7,3},{8,12},{9,13},{10,... | collective-permute-start | bytes 393224 | tf_op jit(solution)/shard_map/ppermute | solution.py:254
  43.0 7.1 %collective-permute-start.10 = (bf16[16,16,128]{2,1,0:T(8,128)(2,1)S(1)}, bf16[16,16,128]{2,1,0:T(8,128)(2,1)S(1)}, u32[]{:S(2)}, u32[]{:S(2)}) collective-permute-start(bf16[16,16,128]{2,1,0:T(8,128)(2,1)S(1)} %add_convert_fusion), channel_id=1, source_target_pairs={{0,8},{1,9},{2,10},{3,11},{4,12},{5,13},{6,14},{7,15},{8,0},{9,1},... | collective-permute-start | bytes 196616 | tf_op jit(solution)/shard_map/ppermute | solution.py:254
  45.7 2.2 %copy-start.3 = (bf16[2048,1024]{1,0:T(8,128)(2,1)S(1)}, bf16[2048,1024]{1,0:T(8,128)(2,1)}, u32[]{:S(2)}) copy-start(bf16[2048,1024]{1,0:T(8,128)(2,1)} %get-tuple-element.13.value_turned) | copy-start | bytes 12582916
  50.1 5.3 %collective-permute-start.11 = (bf16[16,16,128]{2,1,0:T(8,128)(2,1)S(1)}, bf16[16,16,128]{2,1,0:T(8,128)(2,1)S(1)}, u32[]{:S(2)}, u32[]{:S(2)}) collective-permute-start(bf16[16,16,128]{2,1,0:T(8,128)(2,1)S(1)} %collective-permute-done.10), channel_id=1, source_target_pairs={{0,4},{1,5},{2,6},{3,7},{4,0},{5,1},{6,2},{7,3},{8,12},{9,13},{10,... | collective-permute-start | bytes 196616 | tf_op jit(solution)/shard_map/ppermute | solution.py:254
  53.9 5.0 %collective-permute-start.8 = (bf16[16,32,128]{2,1,0:T(8,128)(2,1)S(1)}, bf16[16,32,128]{2,1,0:T(8,128)(2,1)S(1)}, u32[]{:S(2)}, u32[]{:S(2)}) collective-permute-start(bf16[16,32,128]{2,1,0:T(8,128)(2,1)S(1)} %collective-permute-done.7), channel_id=1, source_target_pairs={{0,2},{1,3},{2,0},{3,1},{4,6},{5,7},{6,4},{7,5},{8,10},{9,11},{10,... | collective-permute-start | bytes 393224 | tf_op jit(solution)/shard_map/ppermute | solution.py:254
  55.4 5.2 %copy-start.4 = (bf16[2048,1024]{1,0:T(8,128)(2,1)S(1)}, bf16[2048,1024]{1,0:T(8,128)(2,1)}, u32[]{:S(2)}) copy-start(bf16[2048,1024]{1,0:T(8,128)(2,1)} %get-tuple-element.13.value_turned) | copy-start | bytes 12582916
  55.5 5.0 %collective-permute-start.12 = (bf16[16,32,128]{2,1,0:T(8,128)(2,1)S(1)}, bf16[16,32,128]{2,1,0:T(8,128)(2,1)S(1)}, u32[]{:S(2)}, u32[]{:S(2)}) collective-permute-start(bf16[16,32,128]{2,1,0:T(8,128)(2,1)S(1)} %maximum_select_fusion.2), channel_id=1, source_target_pairs={{0,2},{1,3},{2,0},{3,1},{4,6},{5,7},{6,4},{7,5},{8,10},{9,11},{10,... | collective-permute-start | bytes 393224 | tf_op jit(solution)/shard_map/ppermute | solution.py:254
  58.3 4.6 %collective-permute-start.6 = (bf16[16,64,128]{2,1,0:T(8,128)(2,1)S(1)}, bf16[16,64,128]{2,1,0:T(8,128)(2,1)S(1)}, u32[]{:S(2)}, u32[]{:S(2)}) collective-permute-start(bf16[16,64,128]{2,1,0:T(8,128)(2,1)S(1)} %collective-permute-done.5.rest_1_), channel_id=1, source_target_pairs={{0,1},{1,0},{2,3},{3,2},{4,5},{5,4},{6,7},{7,6},{8,9},{9,8},{10,11... | collective-permute-start | bytes 786440 | tf_op jit(solution)/shard_map/ppermute | solution.py:254
  59.1 3.9 %collective-permute-start.9 = (bf16[16,64,128]{2,1,0:T(8,128)(2,1)S(1)}, bf16[16,64,128]{2,1,0:T(8,128)(2,1)S(1)}, u32[]{:S(2)}, u32[]{:S(2)}) collective-permute-start(bf16[16,64,128]{2,1,0:T(8,128)(2,1)S(1)} %maximum_select_fusion.rest_3_), channel_id=1, source_target_pairs={{0,1},{1,0},{2,3},{3,2},{4,5},{5,4},{6,7},{7,6},{8,9},{9,8},{10,11... | collective-permute-start | bytes 786440 | tf_op jit(solution)/shard_map/ppermute | solution.py:254
  60.6 2.4 %copy-start.2 = (f32[2048]{0:T(1024)S(1)}, f32[2048]{0:T(1024)}, u32[]{:S(2)}) copy-start(f32[2048]{0:T(1024)} %param.13) | copy-start | bytes 24580
  60.6 2.3 %collective-permute-start.13 = (bf16[16,64,128]{2,1,0:T(8,128)(2,1)S(1)}, bf16[16,64,128]{2,1,0:T(8,128)(2,1)S(1)}, u32[]{:S(2)}, u32[]{:S(2)}) collective-permute-start(bf16[16,64,128]{2,1,0:T(8,128)(2,1)S(1)} %maximum_select_fusion.1.rest_5_), channel_id=1, source_target_pairs={{0,1},{1,0},{2,3},{3,2},{4,5},{5,4},{6,7},{7,6},{8,9},{9,8},{10,11... | collective-permute-start | bytes 786440 | tf_op jit(solution)/shard_map/ppermute | solution.py:254

commit v3 on v2

--- a/solution.py
+++ b/solution.py
@@ -10,6 +10,7 @@
 EPSILON = 1e-05
 TILE = 128
 SUB = 8
+RIM = 16
 GROUP = 2
 BF16 = jnp.bfloat16
 F32 = jnp.float32
@@ -43,8 +44,7 @@
 
 def fill(padded, rim, current, column):
     rows, width = current.shape
-    rim_rows = rim.shape[0]
-    padded[SUB - rim_rows : SUB, column : column + width] = rim.astype(F32)
+    padded[0:SUB, column : column + width] = rim.astype(F32)[rim.shape[0] - SUB :]
     padded[SUB : SUB + rows, column : column + width] = current.astype(F32)
 
 
@@ -85,6 +85,13 @@
     put(1 + level_weight.shape[0], jnp.exp(cumul[:, length - 1 :] - cumul))
 
 
+def rim_kernel(query_in, key_in, value_in, rim):
+    width = query_in.shape[1]
+    rim[:, :width] = query_in[...]
+    rim[:, width : 2 * width] = key_in[...]
+    rim[:, 2 * width :] = value_in[...]
+
+
 def prepare_kernel(
     near_count,
     query_in,
@@ -115,7 +122,7 @@
         fill(padded, rim_first[:, width:], key_in[...], width)
         for row in range(0, length, TILE):
             query_tile = conv_tile(padded, weight_first, row, 0, width)
-            query_turned[:, row : row + TILE] = query_tile.T.astype(BF16)
+            query_turned[:, row : row + TILE] = query_tile.astype(BF16).T
             key_tile = conv_tile(padded, weight_first, row, width, width)
             key_out[row : row + TILE, :] = key_tile.astype(BF16)
 
@@ -126,9 +133,11 @@
         at = own * head_width
         for row in range(0, length, TILE):
             tile = conv_tile(padded, weight, row, at, head_width)
-            value_turned[at : at + head_width, row : row + TILE] = tile.T.astype(BF16)
+            value_turned[at : at + head_width, row : row + TILE] = tile.astype(BF16).T
         tail = table[step * group + own, tail_at : tail_at + 1, :]
-        state[own] = dot(scaled(value_turned[at : at + head_width, :], tail), key_out[...])
+        state[own] = dot(
+            scaled(value_turned[at : at + head_width, :], tail), key_out[...]
+        ).astype(BF16)
 
 
 def near_kernel(
@@ -223,6 +232,8 @@
             second = jnp.where(upper, mine, other)
             parts.append(jnp.concatenate([first, second], axis=0))
         states = jnp.concatenate(parts, axis=1)
+        gains = jnp.broadcast_to(gain[:, at : at + head_width], (head_width, head_width)).T
+        gains = jnp.concatenate([gains] * (span // head_width), axis=1)
         head = pl.program_id(0) * group + own
         far_rows = [
             table[own, 1 + near_count + j : 2 + near_count + j, :] * lifts[j, head]
@@ -239,10 +250,8 @@
             )
             total = dot(states, far) + near[at : at + head_width, start : start + span].astype(F32)
             power = jnp.mean(total * total, axis=0, keepdims=True)
-            normed = total * lax.rsqrt(power + EPSILON)
-            output[start : start + span, at : at + head_width] = (
-                normed.T * gain[:, at : at + head_width]
-            ).astype(BF16)
+            normed = total * lax.rsqrt(power + EPSILON) * gains
+            output[start : start + span, at : at + head_width] = normed.astype(BF16).T
 
 
 def whole(shape):
@@ -254,15 +263,18 @@
     return lax.ppermute(x, "seq", [(i, i ^ 1 << bit) for i in range(size)])
 
 
-def climb(state, total, shard_index, seq_bits):
+def climb(state, total, shard_index, seq_bits, beside):
     block = state
     block_total = total
     offset = jnp.zeros_like(total)
+    near = None
     lifts = []
     buckets = []
     for bit in range(seq_bits):
         other = exchange(block.astype(BF16), bit)
         other_total = exchange(block_total, bit)
+        near = beside(bit, near)
+        other, near = lax.optimization_barrier((other, near))
         digit = shard_index >> bit & 1
         upper = digit == 1
         lifts.append(jnp.where(upper, jnp.exp(offset), 0.0))
@@ -273,7 +285,7 @@
             other_part = lax.dynamic_slice_in_dim(other, digit * share, share, 1)
             own_scale = jnp.where(upper, 1.0, jnp.exp(other_total))[:, None, None]
             other_scale = jnp.where(upper, jnp.exp(block_total), 1.0)[:, None, None]
-            block = own_scale * own_part + other_scale * other_part.astype(F32)
+            block = own_scale * own_part.astype(F32) + other_scale * other_part.astype(F32)
             block_total = block_total + other_total
             offset = offset + jnp.where(upper, other_total, 0.0)
     halves = [buckets[0]]
@@ -287,7 +299,7 @@
                 jnp.concatenate([bucket, other], axis=1),
             )
         halves += [bucket, exchange(bucket, 0)]
-    return jnp.stack(lifts), halves
+    return jnp.stack(lifts), halves, near
 
 
 def on_device(
@@ -303,15 +315,24 @@
     seq_bits = bits_of(size)
     near_count = levels - seq_bits
     shard_index = lax.axis_index("seq")
-    rim = jnp.concatenate(
-        [x[length - taps + 1 :] for x in (query_inputs, key_inputs, value_inputs)], axis=1
-    )
+    last = length // RIM - 1
+    rim = pl.pallas_call(
+        rim_kernel,
+        grid=(1,),
+        in_specs=[
+            pl.BlockSpec((RIM, columns), lambda i: (last, 0)) for columns in (width, width, channels)
+        ],
+        out_specs=whole((RIM, 2 * width + channels)),
+        out_shape=jax.ShapeDtypeStruct((RIM, 2 * width + channels), BF16),
+        compiler_params=pltpu.CompilerParams(vmem_limit_bytes=60 * MIB),
+        name="rim",
+    )(query_inputs, key_inputs, value_inputs)
     rim = lax.ppermute(rim, "seq", [(i, i + 1) for i in range(size - 1)])
     total = jnp.sum(log_decay, axis=1)
 
     group_width = GROUP * head_width
     table_count = levels + 2
-    params = pltpu.CompilerParams(vmem_limit_bytes=40 * MIB)
+    params = pltpu.CompilerParams(vmem_limit_bytes=60 * MIB)
     query_turned, key, value_turned, table, state = pl.pallas_call(
         functools.partial(prepare_kernel, near_count),
         grid=(heads // GROUP,),
@@ -319,8 +340,8 @@
             whole((length, width)),
             whole((length, width)),
             pl.BlockSpec((length, group_width), lambda i: (0, i)),
-            pl.BlockSpec((taps - 1, 2 * width), lambda i: (0, 0)),
-            pl.BlockSpec((taps - 1, group_width), lambda i: (0, i + 2 * width // group_width)),
+            pl.BlockSpec((RIM, 2 * width), lambda i: (0, 0)),
+            pl.BlockSpec((RIM, group_width), lambda i: (0, i + 2 * width // group_width)),
             pl.BlockSpec((taps, 2 * width), lambda i: (0, 0)),
             pl.BlockSpec((taps, group_width), lambda i: (0, i + 2 * width // group_width)),
             whole((heads, length)),
@@ -338,7 +359,7 @@
             jax.ShapeDtypeStruct((length, width), BF16),
             jax.ShapeDtypeStruct((channels, length), BF16),
             jax.ShapeDtypeStruct((heads, table_count, length), F32),
-            jax.ShapeDtypeStruct((heads, head_width, width), F32),
+            jax.ShapeDtypeStruct((heads, head_width, width), BF16),
         ],
         scratch_shapes=[pltpu.VMEM((SUB + length, max(group_width, 2 * width)), F32)],
         compiler_params=pltpu.CompilerParams(vmem_limit_bytes=60 * MIB),
@@ -357,11 +378,13 @@
 
     pieces = min(seq_bits, 4)
     piece_heads = heads // pieces
-    near = None
-    for piece in range(pieces):
+
+    def near_piece(piece, near):
+        if piece >= pieces:
+            return near
         first = piece * piece_heads
         chained = [] if near is None else [near]
-        near = pl.pallas_call(
+        return pl.pallas_call(
             functools.partial(near_kernel, near_count),
             grid=(piece_heads,),
             in_specs=[
@@ -384,7 +407,7 @@
             name="near",
         )(query_turned, key, value_turned, table, *chained)
 
-    lifts, buckets = climb(state, total, shard_index, seq_bits)
+    lifts, buckets, near = climb(state, total, shard_index, seq_bits, near_piece)
     digit = (shard_index & 1).astype(jnp.int32).reshape(1)
     return pl.pallas_call(
         functools.partial(far_kernel, near_count),

time: 70.9 us -> 75.3 us (1.062)
  Pallas kernels: 29.5 us -> 43.9 us
  local copies, waits for them, and re-layouts: 4.99 us -> 1.39 us
  waiting for transfers between devices: 12.5 us -> 9.69 us
  starting transfers between devices: 19.1 us -> 17 us
  other arithmetic: 4.02 us -> 2.27 us
    pallas_call x4 -> x5, Pallas kernels: 8.83 us -> 20.5 us  [the longest x4 19 us: near_piece(): pl.pallas_call(functools.partial(near_kernel, near_count), grid=(piece_he...]
    convert_element_type x4 -> x3, other arithmetic: 3.56 us -> 0.39 us  [climb(): other = exchange(block.astype(BF16), bit)]
    pallas_call x1, Pallas kernels: 7.4 us -> 10.1 us  [on_device(): pl.pallas_call(functools.partial(far_kernel, near_count), grid=(heads //...]
    slice x3 -> x0, local copies, waits for them, and re-layouts: 2.18 us -> none  [on_device(): x[length - taps + 1:]]
    ppermute x13, waiting for transfers between devices: 11.7 us -> 9.68 us  [exchange(): return lax.ppermute(x, 'seq', [(i, i ^ 1 << bit) for i in range(size)])]
    ppermute x13, starting transfers between devices: 16.8 us -> 15.1 us  [exchange(): return lax.ppermute(x, 'seq', [(i, i ^ 1 << bit) for i in range(size)])]
    unnamed x16 -> x18, local copies, waits for them, and re-layouts: 2.81 us -> 1.38 us
    reduce_sum x1, other arithmetic: 0.12 us -> 0.96 us  [on_device(): total = jnp.sum(log_decay, axis=1)]
  transfers between devices with their start and end apart: 14 -> 14, of which waited for: 7 -> 6; matrix products, arithmetic and copies ran while one was open for 3% -> 1% of each run, Pallas kernels for 13% -> 45%
where the time goes in v3:
time: 75.3 us; the launch traced here: 74.4 us
  Pallas kernels  43.9 us (58%)
  starting transfers between devices  17 us (23%)
  waiting for transfers between devices  9.69 us (13%)
  other arithmetic  2.27 us (3%)
  local copies, waits for them, and re-layouts  1.39 us (2%)
    pallas_call x4, Pallas kernels, near_piece(): pl.pallas_call(functools.partial(near_kernel, near_count), grid=(piece_he...  19 us
    ppermute x13, starting transfers between devices, exchange(): return lax.ppermute(x, 'seq', [(i, i ^ 1 << bit) for i in range(size)])  15.1 us
    pallas_call x1, Pallas kernels, on_device(): pl.pallas_call(functools.partial(prepare_kernel, near_count), grid=(heads...  13.2 us
    pallas_call x1, Pallas kernels, on_device(): pl.pallas_call(functools.partial(far_kernel, near_count), grid=(heads //...  10.1 us
    ppermute x13, waiting for transfers between devices, exchange(): return lax.ppermute(x, 'seq', [(i, i ^ 1 << bit) for i in range(size)])  9.68 us
    ppermute x1, starting transfers between devices, on_device(): rim = lax.ppermute(rim, 'seq', [(i, i + 1) for i in range(size - 1)])  1.95 us
    pallas_call x1, Pallas kernels, on_device(): pl.pallas_call(rim_kernel, grid=(1,), in_specs=[pl.BlockSpec((RIM, column...  1.51 us
  transfers between devices with their start and end apart: 14, of which 6 were waited for; matrix products, arithmetic and copies ran while one was open for 1% of the time, Pallas kernels for 45%

profile of v3, /device:TPU:0, one launch (start us, length us, event | category | flops | bytes accessed | tf_op | source)
XLA Modules:
  0.0 74.4 jit_solution(1804932013105659225)
XLA Ops:
  0.0 1.0 %reduce_sum.9 = f32[16]{0:T(128)S(1)} reduce(f32[16,1024]{1,0:T(8,128)} %decay.1, f32[]{:T(128)} %constant.3.clone.1), dimensions={1}, to_apply=%region_0.0 | reduce | flops 16368 | bytes 65604 | tf_op jit(solution)/shard_map/reduce_sum | solution.py:331
  1.0 0.5 collective-permute-start.1
  1.5 1.5 %rim.1 = bf16[16,2304]{1,0:T(8,128)(2,1)} custom-call(bf16[1024,128]{1,0:T(8,128)(2,1)} %query_in.3, bf16[1024,128]{1,0:T(8,128)(2,1)} %key_in.3, bf16[1024,2048]{1,0:T(8,128)(2,1)} %value_in.3), custom_call_target="tpu_custom_call" | custom-call | tf_op jit(solution)/shard_map/rim/pallas_call | solution.py:319
  3.0 2.0 %collective-permute-start = (bf16[16,2304]{1,0:T(8,128)(2,1)}, bf16[16,2304]{1,0:T(8,128)(2,1)S(1)}, u32[]{:S(2)}, u32[]{:S(2)}) collective-permute-start(bf16[16,2304]{1,0:T(8,128)(2,1)} %rim.1), channel_id=1, source_target_pairs={{0,1},{1,2},{2,3},{3,4},{4,5},{5,6},{6,7},{7,8},{8,9},{9,10},{10,1... | collective-permute-start | bytes 221192 | tf_op jit(solution)/shard_map/ppermute | solution.py:330
  5.0 0.0 collective-permute-done.1
  5.0 3.0 %collective-permute-start.2 = (f32[16]{0:T(128)S(1)}, f32[16]{0:T(128)S(1)}, u32[]{:S(2)}, u32[]{:S(2)}) collective-permute-start(f32[16]{0:T(128)S(1)} %get-tuple-element.44), channel_id=1, source_target_pairs={{0,2},{1,3},{2,0},{3,1},{4,6},{5,7},{6,4},{7,5},{8,10},{9,11},{10,... | collective-permute-start | bytes 200 | tf_op jit(solution)/shard_map/ppermute | solution.py:263
  8.0 1.5 %collective-permute-done.2 = f32[16]{0:T(128)S(1)} collective-permute-done((f32[16]{0:T(128)S(1)}, f32[16]{0:T(128)S(1)}, u32[]{:S(2)}, u32[]{:S(2)}) %collective-permute-start.2) | collective-permute-done | bytes 96 | tf_op jit(solution)/shard_map/ppermute | solution.py:263
  9.5 2.2 %collective-permute-start.3 = (f32[16]{0:T(128)S(1)}, f32[16]{0:T(128)S(1)}, u32[]{:S(2)}, u32[]{:S(2)}) collective-permute-start(f32[16]{0:T(128)S(1)} %get-tuple-element.50), channel_id=1, source_target_pairs={{0,4},{1,5},{2,6},{3,7},{4,0},{5,1},{6,2},{7,3},{8,12},{9,13},{10,... | collective-permute-start | bytes 200 | tf_op jit(solution)/shard_map/ppermute | solution.py:263
  11.7 0.0 collective-permute-done.rim_first.rim
  11.8 0.6 copy-done.4
  12.4 13.2 %prepare.1 = (bf16[128,1024]{1,0:T(8,128)(2,1)}, bf16[1024,128]{1,0:T(8,128)(2,1)}, bf16[2048,1024]{1,0:T(8,128)(2,1)}, f32[16,17,1024]{2,1,0:T(8,128)}, bf16[16,128,128]{2,1,0:T(8,128)(2,1)}) custom-call(bf16[1024,128]{1,0:T(8,128)(2,1)} %query_in.3, bf16[1024,128]{1,0:T(8,128)(2,1)} %key_in.3, bf16[1024,2048]{1,0:T(8,128)(2,1)} %value_in.3, ...), custom_call_target="tpu_custom_call" | custom-call | tf_op jit(solution)/shard_map/prepare/pallas_call | solution.py:336
  25.6 0.1 collective-permute-start.4
  25.7 0.0 collective-permute-done.3
  25.7 0.0 copy-start.8
  25.7 4.8 %near.4.rest_0_ = bf16[2048,1024]{1,0:T(8,128)(2,1)} custom-call(bf16[128,1024]{1,0:T(8,128)(2,1)} %get-tuple-element.18.query_turned, bf16[1024,128]{1,0:T(8,128)(2,1)} %get-tuple-element.21.key, bf16[2048,1024]{1,0:T(8,128)(2,1)} %get-tuple-element.22.value_turned, f32[16,17,1024]{2,1,0:T(8,128)} %get-tuple-element.19.table), custom_call_target="tpu_custom_call" | custom-call | flops 4294967296 | bytes 2097152 | tf_op jit(solution)/shard_map/near/pallas_call | solution.py:387
  30.5 0.0 collective-permute-done.4.rest_0_
  30.6 0.0 copy-done.8
  30.6 0.2 fusion.8
  30.7 1.5 %collective-permute-start.5 = (bf16[16,64,128]{2,1,0:T(8,128)(2,1)S(1)}, bf16[16,64,128]{2,1,0:T(8,128)(2,1)S(1)}, u32[]{:S(2)}, u32[]{:S(2)}) collective-permute-start(bf16[16,64,128]{2,1,0:T(8,128)(2,1)S(1)} %get-tuple-element.39), channel_id=1, source_target_pairs={{0,2},{1,3},{2,0},{3,1},{4,6},{5,7},{6,4},{7,5},{8,10},{9,11},{10,... | collective-permute-start | bytes 786440 | tf_op jit(solution)/shard_map/ppermute | solution.py:263
  32.3 4.7 %near.5.rest_0_ = bf16[2048,1024]{1,0:T(8,128)(2,1)} custom-call(bf16[128,1024]{1,0:T(8,128)(2,1)} %get-tuple-element.18.query_turned, bf16[1024,128]{1,0:T(8,128)(2,1)} %get-tuple-element.21.key, bf16[2048,1024]{1,0:T(8,128)(2,1)} %get-tuple-element.22.value_turned, f32[16,17,1024]{2,1,0:T(8,128)} %get-tuple-element.19.table, ...), custom_call_target="tpu_custom_call", output_to_operand_aliasing={{}: (4, {})} | custom-call | flops 4294967296 | bytes 2097152 | tf_op jit(solution)/shard_map/near/pallas_call | solution.py:387
  37.0 2.5 %collective-permute-done.5.rest_1_ = bf16[16,64,128]{2,1,0:T(8,128)(2,1)S(1)} collective-permute-done((bf16[16,64,128]{2,1,0:T(8,128)(2,1)S(1)}, bf16[16,64,128]{2,1,0:T(8,128)(2,1)S(1)}, u32[]{:S(2)}, u32[]{:S(2)}) %collective-permute-start.5) | collective-permute-done | bytes 262176 | tf_op jit(solution)/shard_map/ppermute | solution.py:263
  39.5 0.1 fusion.7
  39.6 0.7 collective-permute-start.6
  40.3 4.7 %near.6.rest_0_ = bf16[2048,1024]{1,0:T(8,128)(2,1)} custom-call(bf16[128,1024]{1,0:T(8,128)(2,1)} %get-tuple-element.18.query_turned, bf16[1024,128]{1,0:T(8,128)(2,1)} %get-tuple-element.21.key, bf16[2048,1024]{1,0:T(8,128)(2,1)} %get-tuple-element.22.value_turned, f32[16,17,1024]{2,1,0:T(8,128)} %get-tuple-element.19.table, ...), custom_call_target="tpu_custom_call", output_to_operand_aliasing={{}: (4, {})} | custom-call | flops 4294967296 | bytes 2097152 | tf_op jit(solution)/shard_map/near/pallas_call | solution.py:387
  45.0 0.0 collective-permute-done.6
  45.0 0.1 add_convert_fusion
  45.1 2.7 %collective-permute-start.7 = (bf16[16,16,128]{2,1,0:T(8,128)(2,1)S(1)}, bf16[16,16,128]{2,1,0:T(8,128)(2,1)S(1)}, u32[]{:S(2)}, u32[]{:S(2)}) collective-permute-start(bf16[16,16,128]{2,1,0:T(8,128)(2,1)S(1)} %add_convert_fusion), channel_id=1, source_target_pairs={{0,8},{1,9},{2,10},{3,11},{4,12},{5,13},{6,14},{7,15},{8,0},{9,1},... | collective-permute-start | bytes 196616 | tf_op jit(solution)/shard_map/ppermute | solution.py:263
  47.8 4.7 %near.7 = bf16[2048,1024]{1,0:T(8,128)(2,1)} custom-call(bf16[128,1024]{1,0:T(8,128)(2,1)} %get-tuple-element.18.query_turned, bf16[1024,128]{1,0:T(8,128)(2,1)} %get-tuple-element.21.key, bf16[2048,1024]{1,0:T(8,128)(2,1)} %get-tuple-element.22.value_turned, f32[16,17,1024]{2,1,0:T(8,128)} %get-tuple-element.19.table, ...), custom_call_target="tpu_custom_call", output_to_operand_aliasing={{}: (4, {})} | custom-call | flops 4294967296 | bytes 2097152 | tf_op jit(solution)/shard_map/near/pallas_call | solution.py:387
  52.5 0.0 collective-permute-done.7
  52.5 1.4 %collective-permute-start.11 = (bf16[16,16,128]{2,1,0:T(8,128)(2,1)S(1)}, bf16[16,16,128]{2,1,0:T(8,128)(2,1)S(1)}, u32[]{:S(2)}, u32[]{:S(2)}) collective-permute-start(bf16[16,16,128]{2,1,0:T(8,128)(2,1)S(1)} %collective-permute-done.7), channel_id=1, source_target_pairs={{0,4},{1,5},{2,6},{3,7},{4,0},{5,1},{6,2},{7,3},{8,12},{9,13},{10,... | collective-permute-start | bytes 196616 | tf_op jit(solution)/shard_map/ppermute | solution.py:263
  53.9 1.5 %collective-permute-start.9 = (bf16[16,32,128]{2,1,0:T(8,128)(2,1)S(1)}, bf16[16,32,128]{2,1,0:T(8,128)(2,1)S(1)}, u32[]{:S(2)}, u32[]{:S(2)}) collective-permute-start(bf16[16,32,128]{2,1,0:T(8,128)(2,1)S(1)} %collective-permute-done.6), channel_id=1, source_target_pairs={{0,2},{1,3},{2,0},{3,1},{4,6},{5,7},{6,4},{7,5},{8,10},{9,11},{10,... | collective-permute-start | bytes 393224 | tf_op jit(solution)/shard_map/ppermute | solution.py:263
  55.4 1.4 %collective-permute-done.11 = bf16[16,16,128]{2,1,0:T(8,128)(2,1)S(1)} collective-permute-done((bf16[16,16,128]{2,1,0:T(8,128)(2,1)S(1)}, bf16[16,16,128]{2,1,0:T(8,128)(2,1)S(1)}, u32[]{:S(2)}, u32[]{:S(2)}) %collective-permute-start.11) | collective-permute-done | bytes 65568 | tf_op jit(solution)/shard_map/ppermute | solution.py:263
  56.8 1.4 %collective-permute-start.12 = (bf16[16,32,128]{2,1,0:T(8,128)(2,1)S(1)}, bf16[16,32,128]{2,1,0:T(8,128)(2,1)S(1)}, u32[]{:S(2)}, u32[]{:S(2)}) collective-permute-start(bf16[16,32,128]{2,1,0:T(8,128)(2,1)S(1)} %maximum_select_fusion.2), channel_id=1, source_target_pairs={{0,2},{1,3},{2,0},{3,1},{4,6},{5,7},{6,4},{7,5},{8,10},{9,11},{10,... | collective-permute-start | bytes 393224 | tf_op jit(solution)/shard_map/ppermute | solution.py:263
  58.2 0.0 collective-permute-start.8
  58.2 2.1 %collective-permute-done.9 = bf16[16,32,128]{2,1,0:T(8,128)(2,1)S(1)} collective-permute-done((bf16[16,32,128]{2,1,0:T(8,128)(2,1)S(1)}, bf16[16,32,128]{2,1,0:T(8,128)(2,1)S(1)}, u32[]{:S(2)}, u32[]{:S(2)}) %collective-permute-start.9) | collective-permute-done | bytes 131104 | tf_op jit(solution)/shard_map/ppermute | solution.py:263
  60.3 0.1 maximum_select_fusion.rest_3_
  60.4 0.1 collective-permute-start.10
  60.5 1.4 %collective-permute-done.12 = bf16[16,32,128]{2,1,0:T(8,128)(2,1)S(1)} collective-permute-done((bf16[16,32,128]{2,1,0:T(8,128)(2,1)S(1)}, bf16[16,32,128]{2,1,0:T(8,128)(2,1)S(1)}, u32[]{:S(2)}, u32[]{:S(2)}) %collective-permute-start.12) | collective-permute-done | bytes 131104 | tf_op jit(solution)/shard_map/ppermute | solution.py:263
  61.9 0.1 maximum_select_fusion.1.rest_5_
  62.0 0.1 collective-permute-start.13
  62.1 0.7 pad_maximum_fusion.lifts
  62.7 0.0 collective-permute-done.8.rest_2_
  62.7 0.0 collective-permute-done.10.rest_4_
  62.8 0.8 %collective-permute-done.13.rest_6_ = bf16[16,64,128]{2,1,0:T(8,128)(2,1)S(1)} collective-permute-done((bf16[16,64,128]{2,1,0:T(8,128)(2,1)S(1)}, bf16[16,64,128]{2,1,0:T(8,128)(2,1)S(1)}, u32[]{:S(2)}, u32[]{:S(2)}) %collective-permute-start.13) | collective-permute-done | bytes 262176 | tf_op jit(solution)/shard_map/ppermute | solution.py:263
  63.6 0.0 copy-done.2
  63.6 0.0 copy-done.6
  63.6 0.7 copy-done.7
  64.3 10.1 %far.1 = bf16[1024,2048]{1,0:T(8,128)(2,1)} custom-call(bf16[128,1024]{1,0:T(8,128)(2,1)} %get-tuple-element.18.query_turned, f32[16,17,1024]{2,1,0:T(8,128)} %get-tuple-element.19.table, bf16[2048,1024]{1,0:T(8,128)(2,1)} %near.7, f32[1,2048]{1,0:T(1,128)} %bitcast.9, s32[1]{0:T(128)} %bitcast.1.digit, f32[4,16]{1,0:T(4,128)} %pad_maximum_fusion.lifts, ...), custom_call_target="tpu_custom_call" | custom-call | tf_op jit(solution)/shard_map/far/pallas_call | solution.py:412
  (17 shorter events, 0.1 us)
Async XLA Ops:
  1.0 4.0 %collective-permute-start.1 = (f32[16]{0:T(128)S(1)}, f32[16]{0:T(128)S(1)}, u32[]{:S(2)}, u32[]{:S(2)}) collective-permute-start(f32[16]{0:T(128)S(1)} %reduce_sum.9), channel_id=1, source_target_pairs={{0,1},{1,0},{2,3},{3,2},{4,5},{5,4},{6,7},{7,6},{8,9},{9,8},{10,11... | collective-permute-start | bytes 200 | tf_op jit(solution)/shard_map/ppermute | solution.py:263
  3.0 8.8 %collective-permute-start = (bf16[16,2304]{1,0:T(8,128)(2,1)}, bf16[16,2304]{1,0:T(8,128)(2,1)S(1)}, u32[]{:S(2)}, u32[]{:S(2)}) collective-permute-start(bf16[16,2304]{1,0:T(8,128)(2,1)} %rim.1), channel_id=1, source_target_pairs={{0,1},{1,2},{2,3},{3,4},{4,5},{5,6},{6,7},{7,8},{8,9},{9,10},{10,1... | collective-permute-start | bytes 221192 | tf_op jit(solution)/shard_map/ppermute | solution.py:330
  5.0 4.6 %collective-permute-start.2 = (f32[16]{0:T(128)S(1)}, f32[16]{0:T(128)S(1)}, u32[]{:S(2)}, u32[]{:S(2)}) collective-permute-start(f32[16]{0:T(128)S(1)} %get-tuple-element.44), channel_id=1, source_target_pairs={{0,2},{1,3},{2,0},{3,1},{4,6},{5,7},{6,4},{7,5},{8,10},{9,11},{10,... | collective-permute-start | bytes 200 | tf_op jit(solution)/shard_map/ppermute | solution.py:263
  9.5 16.2 %collective-permute-start.3 = (f32[16]{0:T(128)S(1)}, f32[16]{0:T(128)S(1)}, u32[]{:S(2)}, u32[]{:S(2)}) collective-permute-start(f32[16]{0:T(128)S(1)} %get-tuple-element.50), channel_id=1, source_target_pairs={{0,4},{1,5},{2,6},{3,7},{4,0},{5,1},{6,2},{7,3},{8,12},{9,13},{10,... | collective-permute-start | bytes 200 | tf_op jit(solution)/shard_map/ppermute | solution.py:263
  11.8 0.6 copy-start.4
  25.6 4.9 %collective-permute-start.4 = (bf16[16,128,128]{2,1,0:T(8,128)(2,1)}, bf16[16,128,128]{2,1,0:T(8,128)(2,1)S(1)}, u32[]{:S(2)}, u32[]{:S(2)}) collective-permute-start(bf16[16,128,128]{2,1,0:T(8,128)(2,1)} %get-tuple-element.20), channel_id=1, source_target_pairs={{0,1},{1,0},{2,3},{3,2},{4,5},{5,4},{6,7},{7,6},{8,9},{9,8},{10,11... | collective-permute-start | bytes 1572872 | tf_op jit(solution)/shard_map/ppermute | solution.py:263
  25.7 4.8 %copy-start.8 = (bf16[16,128,128]{2,1,0:T(8,128)(2,1)S(1)}, bf16[16,128,128]{2,1,0:T(8,128)(2,1)}, u32[]{:S(2)}) copy-start(bf16[16,128,128]{2,1,0:T(8,128)(2,1)} %get-tuple-element.20) | copy-start | bytes 1572868
  30.6 6.5 %copy-start = (bf16[16,128,128]{2,1,0:T(8,128)(2,1)}, bf16[16,128,128]{2,1,0:T(8,128)(2,1)S(1)}, u32[]{:S(2)}) copy-start(bf16[16,128,128]{2,1,0:T(8,128)(2,1)S(1)} %collective-permute-done.4.rest_0_) | copy-start | bytes 1572868
  30.7 8.8 %collective-permute-start.5 = (bf16[16,64,128]{2,1,0:T(8,128)(2,1)S(1)}, bf16[16,64,128]{2,1,0:T(8,128)(2,1)S(1)}, u32[]{:S(2)}, u32[]{:S(2)}) collective-permute-start(bf16[16,64,128]{2,1,0:T(8,128)(2,1)S(1)} %get-tuple-element.39), channel_id=1, source_target_pairs={{0,2},{1,3},{2,0},{3,1},{4,6},{5,7},{6,4},{7,5},{8,10},{9,11},{10,... | collective-permute-start | bytes 786440 | tf_op jit(solution)/shard_map/ppermute | solution.py:263
  39.5 18.7 %copy-start.3 = (bf16[16,64,128]{2,1,0:T(8,128)(2,1)}, bf16[16,64,128]{2,1,0:T(8,128)(2,1)S(1)}, u32[]{:S(2)}) copy-start(bf16[16,64,128]{2,1,0:T(8,128)(2,1)S(1)} %collective-permute-done.5.rest_1_) | copy-start | bytes 786436
  39.6 5.4 %collective-permute-start.6 = (bf16[16,32,128]{2,1,0:T(8,128)(2,1)S(1)}, bf16[16,32,128]{2,1,0:T(8,128)(2,1)S(1)}, u32[]{:S(2)}, u32[]{:S(2)}) collective-permute-start(bf16[16,32,128]{2,1,0:T(8,128)(2,1)S(1)} %get-tuple-element.35), channel_id=1, source_target_pairs={{0,4},{1,5},{2,6},{3,7},{4,0},{5,1},{6,2},{7,3},{8,12},{9,13},{10,... | collective-permute-start | bytes 393224 | tf_op jit(solution)/shard_map/ppermute | solution.py:263
  45.1 7.4 %collective-permute-start.7 = (bf16[16,16,128]{2,1,0:T(8,128)(2,1)S(1)}, bf16[16,16,128]{2,1,0:T(8,128)(2,1)S(1)}, u32[]{:S(2)}, u32[]{:S(2)}) collective-permute-start(bf16[16,16,128]{2,1,0:T(8,128)(2,1)S(1)} %add_convert_fusion), channel_id=1, source_target_pairs={{0,8},{1,9},{2,10},{3,11},{4,12},{5,13},{6,14},{7,15},{8,0},{9,1},... | collective-permute-start | bytes 196616 | tf_op jit(solution)/shard_map/ppermute | solution.py:263
  52.5 4.3 %collective-permute-start.11 = (bf16[16,16,128]{2,1,0:T(8,128)(2,1)S(1)}, bf16[16,16,128]{2,1,0:T(8,128)(2,1)S(1)}, u32[]{:S(2)}, u32[]{:S(2)}) collective-permute-start(bf16[16,16,128]{2,1,0:T(8,128)(2,1)S(1)} %collective-permute-done.7), channel_id=1, source_target_pairs={{0,4},{1,5},{2,6},{3,7},{4,0},{5,1},{6,2},{7,3},{8,12},{9,13},{10,... | collective-permute-start | bytes 196616 | tf_op jit(solution)/shard_map/ppermute | solution.py:263
  53.9 6.3 %collective-permute-start.9 = (bf16[16,32,128]{2,1,0:T(8,128)(2,1)S(1)}, bf16[16,32,128]{2,1,0:T(8,128)(2,1)S(1)}, u32[]{:S(2)}, u32[]{:S(2)}) collective-permute-start(bf16[16,32,128]{2,1,0:T(8,128)(2,1)S(1)} %collective-permute-done.6), channel_id=1, source_target_pairs={{0,2},{1,3},{2,0},{3,1},{4,6},{5,7},{6,4},{7,5},{8,10},{9,11},{10,... | collective-permute-start | bytes 393224 | tf_op jit(solution)/shard_map/ppermute | solution.py:263
  56.8 5.0 %collective-permute-start.12 = (bf16[16,32,128]{2,1,0:T(8,128)(2,1)S(1)}, bf16[16,32,128]{2,1,0:T(8,128)(2,1)S(1)}, u32[]{:S(2)}, u32[]{:S(2)}) collective-permute-start(bf16[16,32,128]{2,1,0:T(8,128)(2,1)S(1)} %maximum_select_fusion.2), channel_id=1, source_target_pairs={{0,2},{1,3},{2,0},{3,1},{4,6},{5,7},{6,4},{7,5},{8,10},{9,11},{10,... | collective-permute-start | bytes 393224 | tf_op jit(solution)/shard_map/ppermute | solution.py:263
  58.2 4.5 %collective-permute-start.8 = (bf16[16,64,128]{2,1,0:T(8,128)(2,1)S(1)}, bf16[16,64,128]{2,1,0:T(8,128)(2,1)S(1)}, u32[]{:S(2)}, u32[]{:S(2)}) collective-permute-start(bf16[16,64,128]{2,1,0:T(8,128)(2,1)S(1)} %collective-permute-done.5.rest_1_), channel_id=1, source_target_pairs={{0,1},{1,0},{2,3},{3,2},{4,5},{5,4},{6,7},{7,6},{8,9},{9,8},{10,11... | collective-permute-start | bytes 786440 | tf_op jit(solution)/shard_map/ppermute | solution.py:263
  60.4 3.2 %copy-start.1 = (bf16[16,64,128]{2,1,0:T(8,128)(2,1)}, bf16[16,64,128]{2,1,0:T(8,128)(2,1)S(1)}, u32[]{:S(2)}) copy-start(bf16[16,64,128]{2,1,0:T(8,128)(2,1)S(1)} %maximum_select_fusion.rest_3_) | copy-start | bytes 786436
  60.4 2.4 %collective-permute-start.10 = (bf16[16,64,128]{2,1,0:T(8,128)(2,1)S(1)}, bf16[16,64,128]{2,1,0:T(8,128)(2,1)S(1)}, u32[]{:S(2)}, u32[]{:S(2)}) collective-permute-start(bf16[16,64,128]{2,1,0:T(8,128)(2,1)S(1)} %maximum_select_fusion.rest_3_), channel_id=1, source_target_pairs={{0,1},{1,0},{2,3},{3,2},{4,5},{5,4},{6,7},{7,6},{8,9},{9,8},{10,11... | collective-permute-start | bytes 786440 | tf_op jit(solution)/shard_map/ppermute | solution.py:263
  62.0 1.6 %copy-start.2 = (bf16[16,64,128]{2,1,0:T(8,128)(2,1)}, bf16[16,64,128]{2,1,0:T(8,128)(2,1)S(1)}, u32[]{:S(2)}) copy-start(bf16[16,64,128]{2,1,0:T(8,128)(2,1)S(1)} %maximum_select_fusion.1.rest_5_) | copy-start | bytes 786436
  62.0 1.6 %collective-permute-start.13 = (bf16[16,64,128]{2,1,0:T(8,128)(2,1)S(1)}, bf16[16,64,128]{2,1,0:T(8,128)(2,1)S(1)}, u32[]{:S(2)}, u32[]{:S(2)}) collective-permute-start(bf16[16,64,128]{2,1,0:T(8,128)(2,1)S(1)} %maximum_select_fusion.1.rest_5_), channel_id=1, source_target_pairs={{0,1},{1,0},{2,3},{3,2},{4,5},{5,4},{6,7},{7,6},{8,9},{9,8},{10,11... | collective-permute-start | bytes 786440 | tf_op jit(solution)/shard_map/ppermute | solution.py:263
  62.7 0.8 %copy-start.5 = (bf16[16,64,128]{2,1,0:T(8,128)(2,1)}, bf16[16,64,128]{2,1,0:T(8,128)(2,1)S(1)}, u32[]{:S(2)}) copy-start(bf16[16,64,128]{2,1,0:T(8,128)(2,1)S(1)} %collective-permute-done.8.rest_2_) | copy-start | bytes 786436
  62.7 0.8 %copy-start.6 = (bf16[16,64,128]{2,1,0:T(8,128)(2,1)}, bf16[16,64,128]{2,1,0:T(8,128)(2,1)S(1)}, u32[]{:S(2)}) copy-start(bf16[16,64,128]{2,1,0:T(8,128)(2,1)S(1)} %collective-permute-done.10.rest_4_) | copy-start | bytes 786436
  63.6 0.7 copy-start.7
